TPU v7x, 128 devices: a whole 4x4x4 slice. The times are simulated.
128 devices in a mesh: tp: 16 (over z, y), ep: 8 (over x, core).
Axes of the slice: x: 4, y: 4, z: 4, core: 2. Of those that a mesh axis runs over, the one named last changes fastest.
Arguments:
- attn_out: bfloat16 [16384, 8192], P('ep', 'tp'), may hold values from -6 to 6
- residual: bfloat16 [16384, 7168], P(('ep', 'tp')), may hold values from -6 to 6
- w_out: bfloat16 [8192, 7168], P('tp'), may hold values from -0.0625 to 0.0625
- norm_gain: bfloat16 [7168], replicated, may hold values from 0.5 to 1.5
- router: bfloat16 [7168, 256], P(None, 'tp'), may hold values from -0.0625 to 0.0625
- router_bias: float32 [256], replicated, may hold values from -3 to 3
- choices: int32 [16384, 8], P(('ep', 'tp')), may hold values from 0 to 255, as said below
- w_gate: bfloat16 [16, 7168, 2048], P('tp', None, 'ep'), may hold values from -0.0625 to 0.0625
- w_up: bfloat16 [16, 7168, 2048], P('tp', None, 'ep'), may hold values from -0.0625 to 0.0625
- w_down: bfloat16 [16, 2048, 7168], P('tp', 'ep'), may hold values from -0.125 to 0.125
Outputs:
- hidden_out: bfloat16 [16384, 7168], P(('ep', 'tp'))
- moe_out: bfloat16 [16384, 7168], P(('ep', 'tp'))
- load: float32 [256], replicated
- bias_next: float32 [256], replicated
Inputs may be any that keep to these rules, and one draw needn't show every extreme that they name: `choices`: each row names 8 different experts. Among the rows of one device no expert below 16 is named by more than 2 rows; one such expert is named by exactly 2 rows of every device.
All inputs are finite; a program needn't handle non-finite values.
Results may differ from a plain program's by a relative error of at most 0.034.
Values may be sent and summed in bfloat16 or wider, within the bound.
A program may use at most 128 MiB of HBM per device.

v0:
```python
import jax
import jax.numpy as jnp
from jax import lax
from jax.sharding import PartitionSpec as P

TOP = 8
CAP = 2


norm_eps = 1e-06
route_scale = 2.5
bias_rate = 0.001


def on_device(
    attn_out, residual, w_out, norm_gain, router, router_bias, choices, w_gate, w_up, w_down
):
    tp_count = lax.axis_size("tp")
    ep_count = lax.axis_size("ep")
    tok_rows = residual.shape[0]
    width = residual.shape[1]
    routed = router_bias.shape[0]
    projected = lax.psum_scatter(
        jnp.dot(attn_out, w_out, preferred_element_type=jnp.float32).astype(jnp.bfloat16),
        "tp",
        scatter_dimension=0,
        tiled=True,
    ).astype(jnp.float32)
    hidden_out = (residual.astype(jnp.float32) + projected).astype(jnp.bfloat16)
    stream = hidden_out.astype(jnp.float32)
    scaled = stream * lax.rsqrt(jnp.mean(stream * stream, axis=-1, keepdims=True) + norm_eps)
    normed = (scaled * norm_gain.astype(jnp.float32)).astype(jnp.bfloat16)
    logits = jnp.dot(
        normed, lax.all_gather(router, "tp", axis=1, tiled=True), preferred_element_type=jnp.float32
    )
    scores = jax.nn.sigmoid(logits)
    onehot = choices[:, :, None] == jnp.arange(routed, dtype=jnp.int32)[None, None, :]
    chosen = jnp.sum(jnp.where(onehot, scores[:, None, :], 0.0), axis=-1)
    weights = route_scale * chosen / jnp.sum(chosen, axis=-1, keepdims=True)
    window = onehot[:, :, :tp_count]
    expert_weight = jnp.sum(jnp.where(window, weights[:, :, None], 0.0), axis=1)
    member = jnp.any(window, axis=1).astype(jnp.int32)
    slot_rank = jnp.cumsum(member, axis=0) - member
    slot_ids = jnp.arange(CAP, dtype=jnp.int32)[None, :, None]
    slot_pick = (member.T[:, None, :] == 1) & (slot_rank.T[:, None, :] == slot_ids)
    outgoing = jnp.einsum(
        "wcr,rd->wcd", slot_pick.astype(jnp.bfloat16), normed, preferred_element_type=jnp.float32
    ).astype(jnp.bfloat16)
    landed = lax.all_to_all(outgoing, "tp", split_axis=0, concat_axis=0, tiled=True)
    arrived = lax.all_gather(landed[:, None], "ep", axis=1, tiled=True)
    group_rows = tp_count * CAP
    picked = arrived
    picked = jnp.swapaxes(picked, 0, 1).reshape(lax.axis_size("ep") * group_rows, width)
    gate_val = jnp.dot(picked, w_gate[0], preferred_element_type=jnp.float32)
    up_val = jnp.dot(picked, w_up[0], preferred_element_type=jnp.float32)
    active = (jax.nn.silu(gate_val) * up_val).astype(jnp.bfloat16)
    summed = lax.psum_scatter(
        jnp.dot(active, w_down[0], preferred_element_type=jnp.float32).astype(jnp.bfloat16),
        "ep",
        scatter_dimension=0,
        tiled=True,
    )
    outbound = summed.reshape(tp_count, CAP, width)
    returned = lax.all_to_all(outbound, "tp", split_axis=0, concat_axis=0, tiled=True)
    coeff = jnp.where(slot_pick, expert_weight.T[:, None, :], 0.0)
    mixed = jnp.einsum(
        "wcr,wcd->rd", coeff, returned.astype(jnp.float32), precision=lax.Precision.HIGHEST
    )
    moe_out = mixed.astype(jnp.bfloat16)
    local_counts = jnp.sum(onehot.astype(jnp.int32), axis=(0, 1))
    counts = lax.psum(local_counts, ("tp", "ep"))
    all_slots = tok_rows * tp_count * ep_count * TOP
    load = counts.astype(jnp.float32) * routed / all_slots
    bias_next = router_bias + bias_rate * jnp.sign(all_slots - counts * routed).astype(jnp.float32)
    return (hidden_out, moe_out, load, bias_next)


def solution(mesh):
    placed = (
        P("ep", "tp"),
        P(("ep", "tp"), None),
        P("tp", None),
        P(),
        P(None, "tp"),
        P(),
        P(("ep", "tp"), None),
        P("tp", None, "ep"),
        P("tp", None, "ep"),
        P("tp", "ep", None),
    )
    return jax.shard_map(
        on_device,
        mesh=mesh,
        in_specs=placed,
        out_specs=(P(("ep", "tp"), None), P(("ep", "tp"), None), P(), P()),
        check_vma=False,
    )
```

profile of v0, /device:TPU:1, one launch (start us, length us, event | category | flops | bytes accessed | tf_op | source)
XLA Modules:
  0.0 383.8 jit_solution(6811935811588082357)
XLA Ops:
  7.2 1.5 copy-done
  8.8 22.0 %convolution_convert_fusion = bf16[2048,7168]{1,0:T(8,128)(2,1)} fusion(bf16[2048,512]{1,0:T(8,128)(2,1)S(1)} %copy-done, bf16[512,7168]{1,0:T(8,128)(2,1)} %param.12), kind=kOutput, calls=%fused_computation | convolution fusion | flops 15047065600 | bytes 38797312 | tf_op jit(solution)/shard_map/dot_general | solution.py:24
  30.9 0.6 copy-done.5
  32.1 176.8 %reduce-scatter.3.cloned.1.call-done = bf16[128,7168]{1,0:T(8,128)(2,1)} async-done(((bf16[2048,7168]{1,0:T(8,128)(2,1)}), bf16[128,7168]{1,0:T(8,128)(2,1)}) %reduce-scatter.3.cloned.1.call-update) | async-done | bytes 1835024 | tf_op jit(solution)/shard_map/reduce_scatter | solution.py:23
  208.9 2.2 fusion.1
  211.2 0.7 convolution_convert_fusion.2
  211.9 0.5 copy.49
  212.4 14.9 %all_to_all.10 = bf16[16,2,7168]{2,1,0:T(2,128)(2,1)S(1)} all-to-all(bf16[16,2,7168]{2,1,0:T(2,128)(2,1)S(1)} %copy.49), channel_id=1, replica_groups=mesh['tp'=16,'ep'=8] {'tp'}, dimensions={0} | all-to-all | bytes 917504 | tf_op jit(solution)/shard_map/all_to_all | solution.py:49
  227.2 0.8 copy.50
  228.2 0.7 all-gather.4.cloned.1.call-update
  228.8 0.2 reduce-scatter.5.cloned.1.call-start
  229.1 28.1 %all-gather.6.cloned.1.call-done = bf16[16,16,7168]{2,0,1:T(8,128)(2,1)} async-done(((bf16[16,2,7168]{2,0,1:T(8,128)(2,1)}), bf16[16,16,7168]{2,0,1:T(8,128)(2,1)}) %all-gather.6.cloned.1.call-update) | async-done | bytes 3670032 | tf_op jit(solution)/shard_map/all_gather | solution.py:50
  257.1 7.7 %copy.60 = bf16[16,8,2,7168]{3,2,0,1:T(2,128)(2,1)} copy(bf16[16,8,2,7168]{3,0,2,1:T(8,128)(2,1)} %bitcast.37) | data formatting | bytes 7340032 | tf_op jit(solution)/shard_map/all_gather | solution.py:50
  264.9 8.4 %reshape.48 = bf16[256,7168]{1,0:T(8,128)(2,1)} reshape(bf16[8,16,2,7168]{3,2,1,0:T(2,128)(2,1)} %bitcast.36) | data formatting | bytes 7340032 | tf_op jit(solution)/shard_map/reshape | solution.py:53
  273.3 4.3 %fusion.7 = f32[256,256]{1,0:T(8,128)S(1)} fusion(bf16[256,7168]{1,0:T(8,128)(2,1)} %reshape.48, bf16[1,7168,256]{2,1,0:T(8,128)(2,1)} %param.17), kind=kOutput, calls=%fused_computation.13 | convolution fusion | flops 939524096 | bytes 7602176 | tf_op jit(solution)/shard_map/dot_general | solution.py:54
  277.6 10.1 %convolution_convert_fusion.1 = bf16[256,7168]{1,0:T(8,128)(2,1)} fusion(bf16[1,256,7168]{2,1,0:T(8,128)(2,1)} %param.19, bf16[256,7168]{1,0:T(8,128)(2,1)} %reshape.48, bf16[1,7168,256]{2,1,0:T(8,128)(2,1)} %param.18, f32[256,256]{1,0:T(8,128)S(1)} %fusion.7), kind=kOutput, calls=%fused_computation.1 | convolution fusion | flops 1881276416 | bytes 14942208 | tf_op jit(solution)/shard_map/dot_general | solution.py:58
  287.9 65.8 %psum.7 = s32[256]{0:T(256)S(1)} all-reduce(s32[256]{0:T(256)S(1)} %convert_reduce_fusion), channel_id=1, replica_groups=mesh['tp'=16,'ep'=8] {'tp','ep'}, use_global_device_ids=true, to_apply=%region_9.10 | all-reduce | flops 256 | bytes 2048 | tf_op jit(solution)/shard_map/psum | solution.py:71
  353.7 0.6 multiply_add_fusion
  354.3 4.1 %fusion.20 = f32[128,256]{1,0:T(8,128)S(1)} fusion(bf16[7168,256]{0,1:T(8,128)(2,1)} %all-gather.4.cloned.1.call-done, bf16[128,7168]{1,0:T(8,128)(2,1)} %copy-done.3, f32[7168]{0:T(1024)S(1)} %convert_element_type.56, f32[128]{0:T(128)S(1)} %add_rsqrt_fusion), kind=kOutput, calls=%fused_computation.25 | convolution fusion | flops 473530368 | bytes 5665280 | tf_op jit(solution)/shard_map/dot_general | solution.py:33
  358.5 2.0 reshape.49
  360.5 4.0 %all-to-all-start.1 = ((bf16[16,2,7168]{2,1,0:T(2,128)(2,1)}), bf16[16,2,7168]{2,1,0:T(2,128)(2,1)S(1)}, u32[]{:S(2)}, u32[]{:S(2)}) async-start(bf16[16,2,7168]{2,1,0:T(2,128)(2,1)} %reshape.49), calls=%async_computation.3 | async-start | bytes 917504 | tf_op jit(solution)/shard_map/all_to_all | solution.py:64
  364.5 0.3 select_reduce_fusion.1
  365.1 9.3 %all-to-all-done.1 = bf16[16,2,7168]{2,1,0:T(2,128)(2,1)S(1)} async-done(((bf16[16,2,7168]{2,1,0:T(2,128)(2,1)}), bf16[16,2,7168]{2,1,0:T(2,128)(2,1)S(1)}, u32[]{:S(2)}, u32[]{:S(2)}) %all-to-all-start.1) | async-done | bytes 458784 | tf_op jit(solution)/shard_map/all_to_all | solution.py:64
  374.4 2.9 fusion
  (36 shorter events, 1.4 us)
Async XLA Ops:
  7.2 1.6 copy-start
  7.2 201.7 %reduce-scatter.3.cloned.1.call-start = ((), (), s32[]{:S(2)}) async-start(), calls=%async_computation.4 | async-start | bytes 31195136 | tf_op jit(solution)/shard_map/reduce_scatter | solution.py:23
  30.8 0.7 copy-start.5
  30.8 0.7 copy-start.4
  30.8 178.1 %copy-start.2 = (bf16[128,7168]{1,0:T(8,128)(2,1)S(1)}, bf16[128,7168]{1,0:T(8,128)(2,1)}, u32[]{:S(2)}) copy-start(bf16[128,7168]{1,0:T(8,128)(2,1)} %param.11) | copy-start | bytes 5505028
  30.8 226.3 %all-gather.6.cloned.1.call-start = ((), (), s32[]{:S(2)}) async-start(), calls=%async_computation.7 | async-start | bytes 4128768 | tf_op jit(solution)/shard_map/all_gather | solution.py:50
  211.2 16.1 %copy-start.3 = (bf16[128,7168]{1,0:T(8,128)(2,1)}, bf16[128,7168]{1,0:T(8,128)(2,1)S(1)}, u32[]{:S(2)}) copy-start(bf16[128,7168]{1,0:T(8,128)(2,1)S(1)} %get-tuple-element.7) | copy-start | bytes 5505028
  228.1 126.2 %all-gather.4.cloned.1.call-start = ((), (), s32[]{:S(2)}) async-start(), calls=%async_computation.5 | async-start | bytes 3899392 | tf_op jit(solution)/shard_map/all_gather | solution.py:34
  228.8 129.7 %reduce-scatter.5.cloned.1.call-start = ((), (), s32[]{:S(2)}) async-start(), calls=%async_computation.6 | async-start | bytes 4128768 | tf_op jit(solution)/shard_map/reduce_scatter | solution.py:57
  287.7 66.0 %copy-start.6 = (f32[256]{0:T(256)S(1)}, f32[256]{0:T(256)}, u32[]{:S(2)}) copy-start(f32[256]{0:T(256)} %param.15) | copy-start | bytes 3076
  354.3 23.0 %copy-start.1 = (bf16[2048,512]{1,0:T(8,128)(2,1)S(1)}, bf16[2048,512]{1,0:T(8,128)(2,1)}, u32[]{:S(2)}) copy-start(bf16[2048,512]{1,0:T(8,128)(2,1)} %param.10) | copy-start | bytes 6291460
  360.5 13.9 %all-to-all-start.1 = ((bf16[16,2,7168]{2,1,0:T(2,128)(2,1)}), bf16[16,2,7168]{2,1,0:T(2,128)(2,1)S(1)}, u32[]{:S(2)}, u32[]{:S(2)}) async-start(bf16[16,2,7168]{2,1,0:T(2,128)(2,1)} %reshape.49), calls=%async_computation.3 | async-start | bytes 917504 | tf_op jit(solution)/shard_map/all_to_all | solution.py:64
Sparse Core Ops, SparseCore 0:
  30.9 177.9 reduce-scatter.2
  228.2 28.8 all-gather.5
  259.3 49.6 all-gather.3
  311.3 33.4 reduce-scatter.4
where the time goes:
time: 385 us; the launch traced here: 384 us
  waiting for transfers between devices  215 us (56%)
  blocking collectives  80.7 us (21%)
  matrix products  44.1 us (11%)
  local copies, waits for them, and re-layouts  22.1 us (6%)
  between operations  13.9 us (4%)
  starting transfers between devices  4.38 us (1%)
    reduce_scatter x1, waiting for transfers between devices, on_device(): lax.psum_scatter(jnp.dot(attn_out, w_out, preferred_element_type=jnp.floa...  177 us
    psum x1, blocking collectives, on_device(): counts = lax.psum(local_counts, ('tp', 'ep'))  65.8 us
    all_gather x1, waiting for transfers between devices, on_device(): arrived = lax.all_gather(landed[:, None], 'ep', axis=1, tiled=True)  28.1 us
    dot_general x1, matrix products, on_device(): jnp.dot(attn_out, w_out, preferred_element_type=jnp.float32)  22 us
    all_to_all x1, blocking collectives, on_device(): lax.all_to_all(outgoing, 'tp', split_axis=0, concat_axis=0, tiled=True)  14.9 us
    dot_general x1, matrix products, on_device(): jnp.dot(active, w_down[0], preferred_element_type=jnp.float32)  10.1 us
    all_to_all x1, waiting for transfers between devices, on_device(): lax.all_to_all(outbound, 'tp', split_axis=0, concat_axis=0, tiled=True)  9.26 us
    reshape x1, local copies, waits for them, and re-layouts, on_device(): jnp.swapaxes(picked, 0, 1).reshape(lax.axis_size('ep') * group_rows, width)  8.42 us
  transfers between devices with their start and end apart: 5, of which 3 were waited for; matrix products, arithmetic and copies ran while one was open for 10% of the time, Pallas kernels for 0%

commit v1 on v0

--- a/solution.py
+++ b/solution.py
@@ -1,6 +1,8 @@
 import jax
 import jax.numpy as jnp
 from jax import lax
+from jax.experimental import pallas as pl
+from jax.experimental.pallas import tpu as pltpu
 from jax.sharding import PartitionSpec as P
 
 TOP = 8
@@ -10,6 +12,241 @@
 norm_eps = 1e-06
 route_scale = 2.5
 bias_rate = 0.001
+
+
+MESH = pl.DeviceIdType.MESH
+VMEM = pltpu.VMEM
+ROUNDS = 7
+CH = 256
+
+
+def ring(i):
+    return lax.rem(i + 8, 4)
+
+
+def place():
+    tp = lax.axis_index("tp")
+    ep = lax.axis_index("ep")
+    return lax.div(tp, 4), lax.rem(tp, 4), lax.div(ep, 2), lax.rem(ep, 2)
+
+
+def at(z, y, x, c):
+    return (ring(z) * 4 + ring(y), ring(x) * 2 + lax.rem(c, 2))
+
+
+def greet(peers):
+    barrier = pltpu.get_barrier_semaphore()
+    for peer in peers:
+        pl.semaphore_signal(barrier, inc=1, device_id=peer, device_id_type=MESH)
+    pl.semaphore_wait(barrier, len(peers))
+
+
+def remote(src, dst, send, recv, peer):
+    return pltpu.make_async_remote_copy(
+        src_ref=src, dst_ref=dst, send_sem=send, recv_sem=recv, device_id=peer, device_id_type=MESH
+    )
+
+
+def project_kernel(
+    a_ref, w_ref, res_ref, out_ref,
+    ag, wown, wbuf, pbuf, rbuf, resv,
+    loc, a_s, a_r, y_s, y_r, x_s, x_r, f_s, f_r, c_s, c_r, z_s, z_r,
+):
+    z, y, x, c = place()
+    half = pl.multiple_of(c * 256, 256)
+    own_a = pltpu.make_async_copy(a_ref.at[:, y], ag.at[0], loc.at[0])
+    own_w = pltpu.make_async_copy(w_ref, wown, loc.at[1])
+    own_res = pltpu.make_async_copy(res_ref, resv, loc.at[2])
+    own_a.start()
+    own_w.start()
+    own_res.start()
+    greet(
+        [at(z, y + e, x, c) for e in (1, 2, 3)]
+        + [at(z + e, y, x, c) for e in (1, 2, 3)]
+        + [at(z, y, x + 1, c), at(z, y, x - 1, c), at(z, y, x, c + 1)]
+    )
+    sib = at(z, y, x, c + 1)
+
+    def chunk(dx, r):
+        return ring(x + dx) * ROUNDS + r
+
+    def y_copy(r, e):
+        n = chunk(0, r)
+        cols = pl.ds(pl.multiple_of(n * CH, CH), CH)
+        return remote(
+            w_ref.at[pl.ds(half, 256), cols], wbuf.at[n, 3 - e, pl.ds(half, 256), :],
+            y_s.at[r, e - 1], y_r.at[r, 3 - e], at(z, y + e, x, c),
+        )
+
+    def a_copy(e):
+        return remote(a_ref.at[:, ring(y + e)], ag.at[4 - e], a_s.at[e - 1], a_r.at[3 - e], at(z, y + e, x, c))
+
+    def x_copy(r, way):
+        part = wbuf.at[chunk(0, r), :, pl.ds(half, 256), :]
+        return remote(part, part, x_s.at[r, way], x_r.at[r, way], at(z, y, x + 1 - 2 * way, c))
+
+    def x_land(r, way):
+        part = wbuf.at[chunk(2 * way - 1, r), :, pl.ds(half, 256), :]
+        return remote(part, part, x_s.at[r, way], x_r.at[r, way], at(z, y, x + 1 - 2 * way, c))
+
+    def f_part(dx, r, way):
+        return wbuf.at[chunk(dx, r), :, pl.ds(pl.multiple_of(half + 128 * way, 128), 128), :]
+
+    def f_copy(r, way):
+        part = f_part(2 * way - 1, r, way)
+        return remote(part, part, f_s.at[r, way], f_r.at[r, way], at(z, y, x + 1 - 2 * way, c))
+
+    def f_land(r, way):
+        part = f_part(2, r, way)
+        return remote(part, part, f_s.at[r, way], f_r.at[r, way], at(z, y, x + 1 - 2 * way, c))
+
+    def hop(q):
+        return (0, 3, 1, 2)[q]
+
+    def c_copy(r, q):
+        part = wbuf.at[chunk(hop(q), r), :, pl.ds(half, 256), :]
+        return remote(part, part, c_s.at[r, q], c_r.at[r, q], sib)
+
+    def c_land(n, r, q):
+        other = pl.multiple_of(256 - half, 256)
+        part = wbuf.at[n, :, pl.ds(other, 256), :]
+        return remote(part, part, c_s.at[r, q], c_r.at[r, q], sib)
+
+    def z_copy(n, e):
+        return remote(pbuf.at[n, ring(z + e)], rbuf.at[n, 3 - e], z_s.at[n, e - 1], z_r.at[n, 3 - e], at(z + e, y, x, c))
+
+    def z_land(n, k):
+        return remote(pbuf.at[n, 0], rbuf.at[n, k], z_s.at[n, k], z_r.at[n, k], at(z + 1, y, x, c))
+
+    def y_land(r, k):
+        n = chunk(0, r)
+        part = wbuf.at[n, k, pl.ds(half, 256), :]
+        return remote(part, part, y_s.at[r, k], y_r.at[r, k], at(z, y + 1, x, c))
+
+    def start_y(r):
+        for e in (1, 3, 2):
+            y_copy(r, e).start()
+
+    def first(r):
+        for k in range(3):
+            y_land(r, k).wait_recv()
+        x_copy(r, 0).start()
+        x_copy(r, 1).start()
+        c_copy(r, 0).start()
+
+        @pl.when(r + 2 < ROUNDS)
+        def _():
+            start_y(r + 2)
+
+    def multiply(r):
+        @pl.loop(0, 4)
+        def _(q):
+            dx = q + lax.div(q, 2) - 2 * lax.div(q, 3)
+            slot = q + lax.rem(q, 3) - 3 * lax.div(q, 2) + 3 * lax.div(q, 3)
+            n = chunk(dx, r)
+            c_land(n, r, slot).wait_recv()
+            cols = pl.ds(pl.multiple_of(n * CH, CH), CH)
+            total = jnp.dot(ag[0].reshape(512, 512), wown[:, cols], preferred_element_type=jnp.float32)
+            for k in range(3):
+                total += jnp.dot(ag[k + 1].reshape(512, 512), wbuf[n, k], preferred_element_type=jnp.float32)
+            pbuf[n] = total.astype(jnp.bfloat16).reshape(4, 128, CH)
+            for e in (2, 1, 3):
+                z_copy(n, e).start()
+
+    def finish(r):
+        @pl.loop(0, 4)
+        def _(q):
+            dx = q + lax.div(q, 2) - 2 * lax.div(q, 3)
+            n = chunk(dx, r)
+            for k in range(3):
+                z_land(n, k).wait_recv()
+            cols = pl.ds(pl.multiple_of(n * CH, CH), CH)
+            total = pbuf[n, z].astype(jnp.float32)
+            for k in range(3):
+                total += rbuf[n, k].astype(jnp.float32)
+            out_ref[:, cols] = (resv[:, cols].astype(jnp.float32) + total).astype(jnp.bfloat16)
+
+    start_y(0)
+    for e in (2, 1, 3):
+        a_copy(e).start()
+    start_y(1)
+    first(0)
+    first(1)
+    own_a.wait()
+    own_w.wait()
+    own_res.wait()
+
+    @pl.loop(0, ROUNDS + 4)
+    def _(r):
+        @pl.when(r < ROUNDS)
+        def _():
+            for way in (0, 1):
+                x_land(r, way).wait_recv()
+                f_copy(r, way).start()
+                c_copy(r, 1 + way).start()
+
+        @pl.when(r + 2 < ROUNDS)
+        def _():
+            first(r + 2)
+
+        @pl.when(r == 1)
+        def _():
+            for k in range(3):
+                remote(ag.at[k + 1], ag.at[k + 1], a_s.at[k], a_r.at[k], at(z, y + 1, x, c)).wait_recv()
+
+        @pl.when((r >= 1) & (r <= ROUNDS))
+        def _():
+            for way in (0, 1):
+                f_land(r - 1, way).wait_recv()
+            c_copy(r - 1, 3).start()
+            multiply(r - 1)
+
+        @pl.when(r >= 4)
+        def _():
+            finish(r - 4)
+
+    for e in (1, 2, 3):
+        a_copy(e).wait_send()
+
+    @pl.loop(0, ROUNDS)
+    def _(r):
+        for e in (1, 2, 3):
+            y_copy(r, e).wait_send()
+        for way in (0, 1):
+            x_copy(r, way).wait_send()
+            f_copy(r, way).wait_send()
+        for q in range(4):
+            c_copy(r, q).wait_send()
+
+    @pl.loop(0, 4 * ROUNDS)
+    def _(n):
+        for e in (1, 2, 3):
+            z_copy(n, e).wait_send()
+
+
+def project(attn_out, w_out, residual):
+    dma = pltpu.SemaphoreType.DMA
+    anywhere = pl.BlockSpec(memory_space=pl.ANY)
+    return pl.pallas_call(
+        project_kernel,
+        name="project",
+        out_shape=jax.ShapeDtypeStruct((128, 7168), jnp.bfloat16),
+        in_specs=[anywhere] * 3,
+        out_specs=pl.BlockSpec(memory_space=VMEM),
+        scratch_shapes=[
+            VMEM((4, 4, 128, 512), jnp.bfloat16),
+            VMEM((512, 7168), jnp.bfloat16),
+            VMEM((28, 3, 512, CH), jnp.bfloat16),
+            VMEM((28, 4, 128, CH), jnp.bfloat16),
+            VMEM((28, 3, 128, CH), jnp.bfloat16),
+            VMEM((128, 7168), jnp.bfloat16),
+            dma((3,)), dma((3,)), dma((3,)), dma((7, 3)), dma((7, 3)), dma((7, 2)), dma((7, 2)),
+            dma((7, 2)), dma((7, 2)), dma((7, 4)), dma((7, 4)), dma((28, 3)), dma((28, 3)),
+        ],
+        compiler_params=pltpu.CompilerParams(
+            collective_id=0, has_side_effects=True, vmem_limit_bytes=58 * 1024 * 1024
+        ),
+    )(attn_out.reshape(4, 4, 128, 512), w_out, residual)
 
 
 def on_device(
@@ -20,13 +257,7 @@
     tok_rows = residual.shape[0]
     width = residual.shape[1]
     routed = router_bias.shape[0]
-    projected = lax.psum_scatter(
-        jnp.dot(attn_out, w_out, preferred_element_type=jnp.float32).astype(jnp.bfloat16),
-        "tp",
-        scatter_dimension=0,
-        tiled=True,
-    ).astype(jnp.float32)
-    hidden_out = (residual.astype(jnp.float32) + projected).astype(jnp.bfloat16)
+    hidden_out = project(attn_out, w_out, residual)
     stream = hidden_out.astype(jnp.float32)
     scaled = stream * lax.rsqrt(jnp.mean(stream * stream, axis=-1, keepdims=True) + norm_eps)
     normed = (scaled * norm_gain.astype(jnp.float32)).astype(jnp.bfloat16)

time: 385 us -> 334 us (0.87)
  waiting for transfers between devices: 215 us -> 39.7 us
  Pallas kernels: 0 us -> 147 us
  matrix products: 44.1 us -> 22.9 us
    reduce_scatter x1 -> x0, waiting for transfers between devices: 177 us -> none  [on_device(): lax.psum_scatter(jnp.dot(attn_out, w_out, preferred_element_type=jnp.floa...]
    pallas_call x0 -> x1, Pallas kernels: none -> 147 us  [project(): pl.pallas_call(project_kernel, name='project', out_shape=jax.ShapeDtypeSt...]
    dot_general x1 -> x0, matrix products: 22 us -> none  [on_device(): jnp.dot(attn_out, w_out, preferred_element_type=jnp.float32)]
  transfers between devices with their start and end apart: 5 -> 4, of which waited for: 3 -> 2; matrix products, arithmetic and copies ran while one was open for 10% -> 11% of each run, Pallas kernels for 0% -> 0%
where the time goes in v1:
time: 334 us; the launch traced here: 333 us
  Pallas kernels  147 us (44%)
  blocking collectives  78.5 us (24%)
  waiting for transfers between devices  39.7 us (12%)
  matrix products  22.9 us (7%)
  local copies, waits for them, and re-layouts  21.8 us (7%)
  between operations  13.8 us (4%)
  other arithmetic  4.89 us (1%)
  starting transfers between devices  4.51 us (1%)
    pallas_call x1, Pallas kernels, project(): pl.pallas_call(project_kernel, name='project', out_shape=jax.ShapeDtypeSt...  147 us
    psum x1, blocking collectives, on_device(): counts = lax.psum(local_counts, ('tp', 'ep'))  65.8 us
    all_gather x1, waiting for transfers between devices, on_device(): arrived = lax.all_gather(landed[:, None], 'ep', axis=1, tiled=True)  29.7 us
    all_to_all x1, blocking collectives, on_device(): lax.all_to_all(outgoing, 'tp', split_axis=0, concat_axis=0, tiled=True)  12.7 us
    dot_general x1, matrix products, on_device(): jnp.dot(active, w_down[0], preferred_element_type=jnp.float32)  10.1 us
    all_to_all x1, waiting for transfers between devices, on_device(): lax.all_to_all(outbound, 'tp', split_axis=0, concat_axis=0, tiled=True)  9.24 us
    reshape x1, local copies, waits for them, and re-layouts, on_device(): jnp.swapaxes(picked, 0, 1).reshape(lax.axis_size('ep') * group_rows, width)  8.42 us
    all_gather x1, local copies, waits for them, and re-layouts, on_device(): arrived = lax.all_gather(landed[:, None], 'ep', axis=1, tiled=True)  7.72 us
  transfers between devices with their start and end apart: 4, of which 2 were waited for; matrix products, arithmetic and copies ran while one was open for 11% of the time, Pallas kernels for 0%

profile of v1, /device:TPU:1, one launch (start us, length us, event | category | flops | bytes accessed | tf_op | source)
XLA Modules:
  0.0 332.6 jit_solution(9145929267759599281)
XLA Ops:
  7.2 0.7 convert_element_type.40
  7.9 0.8 iota_compare_fusion
  9.2 146.5 %project.1 = bf16[128,7168]{1,0:T(8,128)(2,1)} custom-call(bf16[4,4,128,512]{3,2,1,0:T(8,128)(2,1)} %bitcast.37, bf16[512,7168]{1,0:T(8,128)(2,1)} %w_ref.1, bf16[128,7168]{1,0:T(8,128)(2,1)} %res_ref.1), custom_call_target="tpu_custom_call" | custom-call | tf_op jit(solution)/shard_map/project/pallas_call | solution.py:230
  155.8 1.9 fusion.1
  157.7 2.2 convolution_convert_fusion.1
  159.9 0.5 copy.49
  160.4 12.7 %all_to_all.10 = bf16[16,2,7168]{2,1,0:T(2,128)(2,1)S(1)} all-to-all(bf16[16,2,7168]{2,1,0:T(2,128)(2,1)S(1)} %copy.49), channel_id=1, replica_groups=mesh['tp'=16,'ep'=8] {'tp'}, dimensions={0} | all-to-all | bytes 917504 | tf_op jit(solution)/shard_map/all_to_all | solution.py:280
  173.1 0.8 copy.50
  174.0 0.7 all-gather.4.cloned.1.call-update
  175.0 29.7 %all-gather.6.cloned.1.call-done = bf16[16,16,7168]{2,0,1:T(8,128)(2,1)} async-done(((bf16[16,2,7168]{2,0,1:T(8,128)(2,1)}), bf16[16,16,7168]{2,0,1:T(8,128)(2,1)}) %all-gather.6.cloned.1.call-update) | async-done | bytes 3670032 | tf_op jit(solution)/shard_map/all_gather | solution.py:281
  204.7 7.7 %copy.60 = bf16[16,8,2,7168]{3,2,0,1:T(2,128)(2,1)} copy(bf16[16,8,2,7168]{3,0,2,1:T(8,128)(2,1)} %bitcast.36) | data formatting | bytes 7340032 | tf_op jit(solution)/shard_map/all_gather | solution.py:281
  212.4 8.4 %reshape.52 = bf16[256,7168]{1,0:T(8,128)(2,1)} reshape(bf16[8,16,2,7168]{3,2,1,0:T(2,128)(2,1)} %bitcast.35) | data formatting | bytes 7340032 | tf_op jit(solution)/shard_map/reshape | solution.py:284
  220.8 4.3 %fusion.7 = f32[256,256]{1,0:T(8,128)S(1)} fusion(bf16[256,7168]{1,0:T(8,128)(2,1)} %reshape.52, bf16[1,7168,256]{2,1,0:T(8,128)(2,1)} %param.17), kind=kOutput, calls=%fused_computation.12 | convolution fusion | flops 939524096 | bytes 7602176 | tf_op jit(solution)/shard_map/dot_general | solution.py:285
  225.1 10.1 %convolution_convert_fusion = bf16[256,7168]{1,0:T(8,128)(2,1)} fusion(bf16[1,256,7168]{2,1,0:T(8,128)(2,1)} %param.19, bf16[256,7168]{1,0:T(8,128)(2,1)} %reshape.52, bf16[1,7168,256]{2,1,0:T(8,128)(2,1)} %param.18, f32[256,256]{1,0:T(8,128)S(1)} %fusion.7), kind=kOutput, calls=%fused_computation | convolution fusion | flops 1881276416 | bytes 14942208 | tf_op jit(solution)/shard_map/dot_general | solution.py:289
  235.3 0.7 copy-done.1
  236.1 65.8 %psum.7 = s32[256]{0:T(256)S(1)} all-reduce(s32[256]{0:T(256)S(1)} %convert_reduce_fusion), channel_id=1, replica_groups=mesh['tp'=16,'ep'=8] {'tp','ep'}, use_global_device_ids=true, to_apply=%region_8.9 | all-reduce | flops 256 | bytes 2048 | tf_op jit(solution)/shard_map/psum | solution.py:302
  301.9 0.6 multiply_add_fusion
  302.5 3.4 %fusion.20 = f32[128,256]{1,0:T(8,128)S(1)} fusion(bf16[7168,256]{0,1:T(8,128)(2,1)} %all-gather.4.cloned.1.call-done, bf16[128,7168]{1,0:T(8,128)(2,1)S(1)} %copy-done, f32[7168]{0:T(1024)S(1)} %convert_element_type.40, f32[128]{0:T(128)S(1)} %add_rsqrt_fusion), kind=kOutput, calls=%fused_computation.23 | convolution fusion | flops 473530368 | bytes 5665280 | tf_op jit(solution)/shard_map/dot_general | solution.py:264
  306.0 2.0 reshape.53
  308.0 4.2 %all-to-all-start.1 = ((bf16[16,2,7168]{2,1,0:T(2,128)(2,1)}), bf16[16,2,7168]{2,1,0:T(2,128)(2,1)S(1)}, u32[]{:S(2)}, u32[]{:S(2)}) async-start(bf16[16,2,7168]{2,1,0:T(2,128)(2,1)} %reshape.53), calls=%async_computation.2 | async-start | bytes 917504 | tf_op jit(solution)/shard_map/all_to_all | solution.py:295
  312.2 0.3 select_reduce_fusion.1
  312.8 9.2 %all-to-all-done.1 = bf16[16,2,7168]{2,1,0:T(2,128)(2,1)S(1)} async-done(((bf16[16,2,7168]{2,1,0:T(2,128)(2,1)}), bf16[16,2,7168]{2,1,0:T(2,128)(2,1)S(1)}, u32[]{:S(2)}, u32[]{:S(2)}) %all-to-all-start.1) | async-done | bytes 458784 | tf_op jit(solution)/shard_map/all_to_all | solution.py:295
  322.0 2.9 fusion
  324.9 1.2 copy.62
  (26 shorter events, 1.4 us)
Async XLA Ops:
  7.2 197.5 %all-gather.6.cloned.1.call-start = ((), (), s32[]{:S(2)}) async-start(), calls=%async_computation.5 | async-start | bytes 4128768 | tf_op jit(solution)/shard_map/all_gather | solution.py:281
  174.0 128.5 %all-gather.4.cloned.1.call-start = ((), (), s32[]{:S(2)}) async-start(), calls=%async_computation.3 | async-start | bytes 3899392 | tf_op jit(solution)/shard_map/all_gather | solution.py:265
  174.8 131.3 %reduce-scatter.2.cloned.1.call-start = ((), (), s32[]{:S(2)}) async-start(), calls=%async_computation.4 | async-start | bytes 4128768 | tf_op jit(solution)/shard_map/reduce_scatter | solution.py:288
  235.2 0.7 copy-start.1
  235.2 66.7 %copy-start.2 = (f32[256]{0:T(256)S(1)}, f32[256]{0:T(256)}, u32[]{:S(2)}) copy-start(f32[256]{0:T(256)} %param.15) | copy-start | bytes 3076
  235.2 67.3 %copy-start = (bf16[128,7168]{1,0:T(8,128)(2,1)S(1)}, bf16[128,7168]{1,0:T(8,128)(2,1)}, u32[]{:S(2)}) copy-start(bf16[128,7168]{1,0:T(8,128)(2,1)} %project.1) | copy-start | bytes 5505028
  308.0 14.0 %all-to-all-start.1 = ((bf16[16,2,7168]{2,1,0:T(2,128)(2,1)}), bf16[16,2,7168]{2,1,0:T(2,128)(2,1)S(1)}, u32[]{:S(2)}, u32[]{:S(2)}) async-start(bf16[16,2,7168]{2,1,0:T(2,128)(2,1)} %reshape.53), calls=%async_computation.2 | async-start | bytes 917504 | tf_op jit(solution)/shard_map/all_to_all | solution.py:295
Sparse Core Ops, SparseCore 0:
  174.1 30.4 all-gather.5
  206.8 49.7 all-gather.3
  259.0 33.0 reduce-scatter.1

commit v2 on v1

--- a/solution.py
+++ b/solution.py
@@ -6,7 +6,6 @@
 from jax.sharding import PartitionSpec as P
 
 TOP = 8
-CAP = 2
 
 
 norm_eps = 1e-06
@@ -249,60 +248,340 @@
     )(attn_out.reshape(4, 4, 128, 512), w_out, residual)
 
 
+LANE = 896
+GROUPS = ((0, 0), (1, 1), (2, 3), (3, 2))
+
+
+def moe_kernel(
+    hid_ref, gain_ref, rout_ref, bias_ref, cho_ref, wg_ref, wu_ref, wd_ref,
+    moe_ref, load_ref, next_ref,
+    wg, wu, wd, rt, normed, snd, land, rows, ybuf, r1, sbuf, r2, rsend, ret, cnt, cnt_tp, cnt_ep,
+    loc, d_s, d_r, ax_s, ax_r, ac_s, ac_r, k_s, k_r, l_s, l_r, rt_s, rt_r, rs_s, rs_r,
+    p_s, p_r, q_s, q_r, b_s, b_r,
+):
+    z, y, x, c = place()
+    tp = z * 4 + y
+    ep = x * 2 + c
+    sib = at(z, y, x, c + 1)
+    width = hid_ref.shape[1]
+    half = pl.ds(pl.multiple_of(c * (width // 2), width // 2), width // 2)
+    loads = [pltpu.make_async_copy(s, d, loc.at[i]) for i, (s, d) in enumerate(((wg_ref, wg), (wu_ref, wu), (wd_ref, wd)))]
+    for load in loads:
+        load.start()
+    tp_peers = [(dz, dy) for dz in (0, 1, 3, 2) for dy in (1, 3, 2, 0) if (dz, dy) != (0, 0)]
+    ep_peers = [(dx, dc) for dx in (0, 1, 3, 2) for dc in (0, 1) if (dx, dc) != (0, 0)]
+
+    def tp_at(dz, dy):
+        return ring(z + dz) * 4 + ring(y + dy)
+
+    def ep_at(dx, dc):
+        return ring(x + dx) * 2 + lax.rem(c + dc, 2)
+
+    barrier = pltpu.get_barrier_semaphore()
+    for p in tp_peers:
+        pl.semaphore_signal(barrier, inc=1, device_id=(tp_at(*p), ep), device_id_type=MESH)
+    for p in ep_peers:
+        pl.semaphore_signal(barrier, inc=1, device_id=(tp, ep_at(*p)), device_id_type=MESH)
+
+    def cut(j):
+        return slice(j * LANE, (j + 1) * LANE)
+
+    ssq = jnp.zeros((128, 1), jnp.float32)
+    for j in range(8):
+        h = hid_ref[:, cut(j)].astype(jnp.float32)
+        ssq += jnp.sum(h * h, axis=1, keepdims=True)
+    scale = lax.rsqrt(ssq / width + norm_eps)
+    for j in range(8):
+        h = hid_ref[:, cut(j)].astype(jnp.float32)
+        normed[:, cut(j)] = (h * scale * gain_ref[:, cut(j)].astype(jnp.float32)).astype(jnp.bfloat16)
+
+    row = lax.broadcasted_iota(jnp.int32, (256, 128), 0)
+    lane = lax.broadcasted_iota(jnp.int32, (256, 128), 1)
+    expert = row // 16
+    member = jnp.zeros((256, 128), jnp.float32)
+    named = jnp.zeros((256, 128), jnp.float32)
+    for k in range(TOP):
+        ck = cho_ref[k : k + 1, :]
+        member += jnp.where(ck == expert, 1.0, 0.0)
+        named += jnp.where(ck == row, 1.0, 0.0)
+    before = jnp.where(row[:128] < lane[:128], 1.0, 0.0).astype(jnp.bfloat16)
+    rank = jnp.dot(member.astype(jnp.bfloat16), before, preferred_element_type=jnp.float32)
+    slot = ((row // 8) % 2).astype(jnp.float32)
+    pick = jnp.where(rank == slot, member, 0.0)
+    feature = row % 8
+    outgoing = jnp.zeros((256, LANE), jnp.float32)
+    for j in range(8):
+        pj = jnp.where(feature == j, pick, 0.0).astype(jnp.bfloat16)
+        outgoing += jnp.dot(pj, normed[:, cut(j)], preferred_element_type=jnp.float32)
+    snd[...] = outgoing.astype(jnp.bfloat16).reshape(16, 16, LANE)
+    contract_last = (((1,), (1,)), ((), ()))
+    cnt[...] = lax.dot_general(
+        jnp.ones((8, 128), jnp.bfloat16), named.astype(jnp.bfloat16), contract_last, preferred_element_type=jnp.float32
+    )
+    pl.semaphore_wait(barrier, len(tp_peers) + len(ep_peers))
+
+    def d_copy(p):
+        peer = tp_at(*p)
+        return remote(snd.at[peer], land.at[ep, tp], d_s.at[peer], d_r.at[tp], (peer, ep))
+
+    own_rows = pltpu.make_async_copy(snd.at[tp], land.at[ep, tp], loc.at[3])
+    own_rows.start()
+    for p in tp_peers:
+        d_copy(p).start()
+
+    def k_copy(p):
+        peer = tp_at(*p)
+        return remote(cnt, cnt_tp.at[tp], k_s.at[peer], k_r.at[tp], (peer, ep))
+
+    for p in tp_peers:
+        k_copy(p).start()
+
+    def group(dz):
+        return pl.ds(pl.multiple_of(ring(z + dz) * 4, 4), 4)
+
+    def x_copy(g, dz, e):
+        part = land.at[ep, group(dz)]
+        return remote(part, part, ax_s.at[g, e - 1], ax_r.at[g, 3 - e], (tp, ep_at(e, 0)))
+
+    def x_land(g, dz, k):
+        part = land.at[ep_at(k + 1, 0), group(dz)]
+        return remote(part, part, ax_s.at[g, k], ax_r.at[g, k], (tp, ep_at(1, 0)))
+
+    def c_copy(g, dz, q):
+        part = land.at[ep_at(q, 0), group(dz)]
+        return remote(part, part, ac_s.at[g, q], ac_r.at[g, q], sib)
+
+    def c_land(g, dz, q):
+        part = land.at[ep_at(q, 1), group(dz)]
+        return remote(part, part, ac_s.at[g, q], ac_r.at[g, q], sib)
+
+    def d_land(p):
+        src = tp_at(*p)
+        return remote(snd.at[src], land.at[ep, src], d_s.at[src], d_r.at[src], (src, ep))
+
+    for g, dz in GROUPS:
+        for p in tp_peers:
+            if p[0] == dz:
+                d_land(p).wait_recv()
+        if dz == 0:
+            own_rows.wait()
+        for e in (1, 3, 2):
+            x_copy(g, dz, e).start()
+        c_copy(g, dz, 0).start()
+
+    def rt_copy(p):
+        peer = tp_at(*p)
+        return remote(rout_ref.at[:, half], rt.at[tp, :, half], rt_s.at[peer], rt_r.at[tp], (peer, ep))
+
+    own_rt = pltpu.make_async_copy(rout_ref.at[:, half], rt.at[tp, :, half], loc.at[4])
+    own_rt.start()
+    for p in tp_peers:
+        rt_copy(p).start()
+
+    for p in tp_peers:
+        src = tp_at(*p)
+        remote(cnt, cnt_tp.at[src], k_s.at[src], k_r.at[src], (src, ep)).wait_recv()
+    cnt_tp[tp] = cnt[...]
+    part_sum = cnt_tp[0]
+    for i in range(1, 16):
+        part_sum += cnt_tp[i]
+    cnt_ep[ep] = part_sum
+
+    def l_copy(p):
+        peer = ep_at(*p)
+        return remote(cnt_ep.at[ep], cnt_ep.at[ep], l_s.at[peer], l_r.at[ep], (tp, peer))
+
+    for p in ep_peers:
+        l_copy(p).start()
+
+    for g, dz in GROUPS:
+        for k in (0, 2, 1):
+            x_land(g, dz, k).wait_recv()
+            c_copy(g, dz, k + 1).start()
+    for g, dz in GROUPS:
+        for q in range(4):
+            c_land(g, dz, q).wait_recv()
+    out_row = lax.broadcasted_iota(jnp.int32, (128, 128), 0)
+    in_row = lax.broadcasted_iota(jnp.int32, (128, 128), 1)
+    source = ((out_row % 16) // 2) * 16 + (out_row % 2) * 8 + out_row // 16
+    perm = jnp.where(in_row == source, 1.0, 0.0).astype(jnp.bfloat16)
+
+    @pl.loop(0, 16)
+    def _(i):
+        group_of, part = lax.div(i, 2), lax.rem(i, 2)
+        block = land[group_of, pl.ds(pl.multiple_of(part * 8, 8), 8)].reshape(128, LANE)
+        turned = jnp.dot(perm, block, preferred_element_type=jnp.float32).astype(jnp.bfloat16)
+        rows[:, pl.ds(pl.multiple_of(i * 16, 16), 16), :] = turned.reshape(8, 16, LANE)
+
+    for load in loads:
+        load.wait()
+    gate_val = jnp.zeros((256, 256), jnp.float32)
+    up_val = jnp.zeros((256, 256), jnp.float32)
+    for j in range(8):
+        gate_val += jnp.dot(rows[j], wg[cut(j), :], preferred_element_type=jnp.float32)
+        up_val += jnp.dot(rows[j], wu[cut(j), :], preferred_element_type=jnp.float32)
+    active = (gate_val / (1.0 + jnp.exp(-gate_val)) * up_val).astype(jnp.bfloat16)
+
+    def p_copy(n):
+        return remote(ybuf.at[n, :, 1 - c], r1.at[n], p_s.at[n], p_r.at[n], sib)
+
+    def q_copy(n, e):
+        return remote(sbuf.at[n, ring(x + e)], r2.at[n, 3 - e], q_s.at[n, e - 1], q_r.at[n, 3 - e], (tp, ep_at(e, 0)))
+
+    def q_land(n, k):
+        return remote(r2.at[n, k], r2.at[n, k], q_s.at[n, k], q_r.at[n, k], (tp, ep_at(1, 0)))
+
+    for n in range(4):
+        part = jnp.dot(active, wd[:, n * 2 * LANE : (n + 1) * 2 * LANE], preferred_element_type=jnp.float32)
+        ybuf[n] = part.astype(jnp.bfloat16).reshape(4, 2, 32, 2 * LANE)
+        p_copy(n).start()
+    for n in range(4):
+        p_copy(n).wait_recv()
+        for i in range(4):
+            both = ybuf[n, i, c].astype(jnp.float32) + r1[n, i].astype(jnp.float32)
+            sbuf[n, i] = both.astype(jnp.bfloat16)
+        for e in (1, 3, 2):
+            q_copy(n, e).start()
+
+    for p in ep_peers:
+        peer = ep_at(*p)
+        remote(cnt_ep.at[peer], cnt_ep.at[peer], l_s.at[peer], l_r.at[peer], (tp, peer)).wait_recv()
+    counts = cnt_ep[0]
+    for i in range(1, 8):
+        counts += cnt_ep[i]
+    counts = counts[0:1]
+    slots = 128.0 * 128.0 * TOP
+    load_ref[...] = counts * 256.0 / slots
+    gap = slots - counts * 256.0
+    sign = jnp.where(gap > 0.0, 1.0, jnp.where(gap < 0.0, -1.0, 0.0))
+    next_ref[...] = bias_ref[...] + bias_rate * sign
+
+    for p in tp_peers:
+        src = tp_at(*p)
+        remote(rout_ref.at[:, half], rt.at[src, :, half], rt_s.at[src], rt_r.at[src], (src, ep)).wait_recv()
+    own_rt.wait()
+    mine = rt.at[:, :, half]
+    rt_sib = remote(mine, mine, rs_s.at[0], rs_r.at[0], sib)
+    rt_sib.start()
+    other = rt.at[:, :, pl.ds(pl.multiple_of((1 - c) * (width // 2), width // 2), width // 2)]
+    remote(other, other, rs_s.at[0], rs_r.at[0], sib).wait_recv()
+    logits = jnp.zeros((256, 128), jnp.float32)
+    for j in range(8):
+        logits += lax.dot_general(
+            rt[:, :, cut(j)].reshape(256, LANE), normed[:, cut(j)], contract_last, preferred_element_type=jnp.float32
+        )
+    scores = 1.0 / (1.0 + jnp.exp(-logits))
+    chosen = []
+    for k in range(TOP):
+        hit = cho_ref[k : k + 1, :] == row
+        chosen.append(jnp.sum(jnp.where(hit, scores, 0.0), axis=0, keepdims=True))
+    norm_by = chosen[0]
+    for k in range(1, TOP):
+        norm_by = norm_by + chosen[k]
+    weight = jnp.zeros((256, 128), jnp.float32)
+    for k in range(TOP):
+        weight += jnp.where(cho_ref[k : k + 1, :] == expert, route_scale * chosen[k] / norm_by, 0.0)
+    coeff = jnp.where(pick > 0.0, weight, 0.0).T
+    lane_cut = lax.broadcasted_iota(jnp.int32, (128, 256), 1) % 8
+
+    back_row = lax.broadcasted_iota(jnp.int32, (256, 32), 0)
+    back_col = lax.broadcasted_iota(jnp.int32, (256, 32), 1)
+    returned = jnp.zeros((256, LANE), jnp.float32)
+    for n in range(4):
+        for k in (0, 2, 1):
+            q_land(n, k).wait_recv()
+        total = sbuf[n, x].astype(jnp.float32)
+        for k in range(3):
+            total += r2[n, k].astype(jnp.float32)
+        total = total.astype(jnp.bfloat16)
+        for i in range(2):
+            turn = jnp.where((back_row // 8 == back_col) & (back_row % 8 == 2 * n + i), 1.0, 0.0).astype(jnp.bfloat16)
+            returned += jnp.dot(turn, total[:, cut(i)], preferred_element_type=jnp.float32)
+    rsend[...] = returned.astype(jnp.bfloat16).reshape(16, 16, LANE)
+
+    def b_copy(p):
+        peer = tp_at(*p)
+        return remote(rsend.at[peer], ret.at[tp], b_s.at[peer], b_r.at[tp], (peer, ep))
+
+    own_back = pltpu.make_async_copy(rsend.at[tp], ret.at[tp], loc.at[5])
+    own_back.start()
+    for p in tp_peers:
+        b_copy(p).start()
+    high = coeff.astype(jnp.bfloat16)
+    low = (coeff - high.astype(jnp.float32)).astype(jnp.bfloat16)
+    own_back.wait()
+    for p in tp_peers:
+        src = tp_at(*p)
+        remote(rsend.at[src], ret.at[src], b_s.at[src], b_r.at[src], (src, ep)).wait_recv()
+    back = ret[...].reshape(256, LANE)
+    for j in range(8):
+        mixed = jnp.dot(jnp.where(lane_cut == j, high, 0.0).astype(jnp.bfloat16), back, preferred_element_type=jnp.float32)
+        mixed += jnp.dot(jnp.where(lane_cut == j, low, 0.0).astype(jnp.bfloat16), back, preferred_element_type=jnp.float32)
+        moe_ref[:, cut(j)] = mixed.astype(jnp.bfloat16)
+
+    for p in tp_peers:
+        d_copy(p).wait_send()
+        k_copy(p).wait_send()
+        rt_copy(p).wait_send()
+        b_copy(p).wait_send()
+    for p in ep_peers:
+        l_copy(p).wait_send()
+    rt_sib.wait_send()
+    for g, dz in GROUPS:
+        for e in (1, 2, 3):
+            x_copy(g, dz, e).wait_send()
+        for q in range(4):
+            c_copy(g, dz, q).wait_send()
+    for n in range(4):
+        p_copy(n).wait_send()
+        for e in (1, 2, 3):
+            q_copy(n, e).wait_send()
+
+
+def experts(hidden_out, norm_gain, router, router_bias, choices, w_gate, w_up, w_down):
+    dma = pltpu.SemaphoreType.DMA
+    bf16, f32 = jnp.bfloat16, jnp.float32
+    vmem = pl.BlockSpec(memory_space=VMEM)
+    anywhere = pl.BlockSpec(memory_space=pl.ANY)
+    moe_out, load, bias_next = pl.pallas_call(
+        moe_kernel,
+        name="experts",
+        out_shape=(
+            jax.ShapeDtypeStruct((128, 7168), bf16),
+            jax.ShapeDtypeStruct((1, 256), f32),
+            jax.ShapeDtypeStruct((1, 256), f32),
+        ),
+        in_specs=[vmem] * 5 + [anywhere] * 3,
+        out_specs=(vmem,) * 3,
+        scratch_shapes=[
+            VMEM((7168, 256), bf16), VMEM((7168, 256), bf16), VMEM((256, 7168), bf16),
+            VMEM((16, 16, 7168), bf16), VMEM((128, 7168), bf16), VMEM((16, 16, LANE), bf16),
+            VMEM((8, 16, 16, LANE), bf16), VMEM((8, 256, LANE), bf16),
+            VMEM((4, 4, 2, 32, 2 * LANE), bf16), VMEM((4, 4, 32, 2 * LANE), bf16),
+            VMEM((4, 4, 32, 2 * LANE), bf16), VMEM((4, 3, 32, 2 * LANE), bf16),
+            VMEM((16, 16, LANE), bf16), VMEM((16, 16, LANE), bf16),
+            VMEM((8, 256), f32), VMEM((16, 8, 256), f32), VMEM((8, 8, 256), f32),
+            dma((6,)), dma((16,)), dma((16,)), dma((4, 3)), dma((4, 3)), dma((4, 4)), dma((4, 4)),
+            dma((16,)), dma((16,)), dma((8,)), dma((8,)), dma((16,)), dma((16,)), dma((1,)), dma((1,)),
+            dma((4,)), dma((4,)), dma((4, 3)), dma((4, 3)), dma((16,)), dma((16,)),
+        ],
+        compiler_params=pltpu.CompilerParams(
+            collective_id=1, has_side_effects=True, vmem_limit_bytes=56 * 1024 * 1024
+        ),
+    )(
+        hidden_out, norm_gain.reshape(1, -1), router.T, router_bias.reshape(1, -1), choices.T,
+        w_gate[0], w_up[0], w_down[0],
+    )
+    return moe_out, load.reshape(-1), bias_next.reshape(-1)
+
+
 def on_device(
     attn_out, residual, w_out, norm_gain, router, router_bias, choices, w_gate, w_up, w_down
 ):
-    tp_count = lax.axis_size("tp")
-    ep_count = lax.axis_size("ep")
-    tok_rows = residual.shape[0]
-    width = residual.shape[1]
-    routed = router_bias.shape[0]
     hidden_out = project(attn_out, w_out, residual)
-    stream = hidden_out.astype(jnp.float32)
-    scaled = stream * lax.rsqrt(jnp.mean(stream * stream, axis=-1, keepdims=True) + norm_eps)
-    normed = (scaled * norm_gain.astype(jnp.float32)).astype(jnp.bfloat16)
-    logits = jnp.dot(
-        normed, lax.all_gather(router, "tp", axis=1, tiled=True), preferred_element_type=jnp.float32
+    moe_out, load, bias_next = experts(
+        hidden_out, norm_gain, router, router_bias, choices, w_gate, w_up, w_down
     )
-    scores = jax.nn.sigmoid(logits)
-    onehot = choices[:, :, None] == jnp.arange(routed, dtype=jnp.int32)[None, None, :]
-    chosen = jnp.sum(jnp.where(onehot, scores[:, None, :], 0.0), axis=-1)
-    weights = route_scale * chosen / jnp.sum(chosen, axis=-1, keepdims=True)
-    window = onehot[:, :, :tp_count]
-    expert_weight = jnp.sum(jnp.where(window, weights[:, :, None], 0.0), axis=1)
-    member = jnp.any(window, axis=1).astype(jnp.int32)
-    slot_rank = jnp.cumsum(member, axis=0) - member
-    slot_ids = jnp.arange(CAP, dtype=jnp.int32)[None, :, None]
-    slot_pick = (member.T[:, None, :] == 1) & (slot_rank.T[:, None, :] == slot_ids)
-    outgoing = jnp.einsum(
-        "wcr,rd->wcd", slot_pick.astype(jnp.bfloat16), normed, preferred_element_type=jnp.float32
-    ).astype(jnp.bfloat16)
-    landed = lax.all_to_all(outgoing, "tp", split_axis=0, concat_axis=0, tiled=True)
-    arrived = lax.all_gather(landed[:, None], "ep", axis=1, tiled=True)
-    group_rows = tp_count * CAP
-    picked = arrived
-    picked = jnp.swapaxes(picked, 0, 1).reshape(lax.axis_size("ep") * group_rows, width)
-    gate_val = jnp.dot(picked, w_gate[0], preferred_element_type=jnp.float32)
-    up_val = jnp.dot(picked, w_up[0], preferred_element_type=jnp.float32)
-    active = (jax.nn.silu(gate_val) * up_val).astype(jnp.bfloat16)
-    summed = lax.psum_scatter(
-        jnp.dot(active, w_down[0], preferred_element_type=jnp.float32).astype(jnp.bfloat16),
-        "ep",
-        scatter_dimension=0,
-        tiled=True,
-    )
-    outbound = summed.reshape(tp_count, CAP, width)
-    returned = lax.all_to_all(outbound, "tp", split_axis=0, concat_axis=0, tiled=True)
-    coeff = jnp.where(slot_pick, expert_weight.T[:, None, :], 0.0)
-    mixed = jnp.einsum(
-        "wcr,wcd->rd", coeff, returned.astype(jnp.float32), precision=lax.Precision.HIGHEST
-    )
-    moe_out = mixed.astype(jnp.bfloat16)
-    local_counts = jnp.sum(onehot.astype(jnp.int32), axis=(0, 1))
-    counts = lax.psum(local_counts, ("tp", "ep"))
-    all_slots = tok_rows * tp_count * ep_count * TOP
-    load = counts.astype(jnp.float32) * routed / all_slots
-    bias_next = router_bias + bias_rate * jnp.sign(all_slots - counts * routed).astype(jnp.float32)
     return (hidden_out, moe_out, load, bias_next)
 
 

time: 334 us -> 230 us (0.69)
  blocking collectives: 78.5 us -> 0 us
  Pallas kernels: 147 us -> 223 us
  waiting for transfers between devices: 39.7 us -> 0 us
  matrix products: 22.9 us -> 0 us
  local copies, waits for them, and re-layouts: 21.8 us -> 5.85 us
  between operations: 13.8 us -> 0.67 us
  other arithmetic: 4.89 us -> 0 us
  starting transfers between devices: 4.51 us -> 0 us
    pallas_call x0 -> x1, Pallas kernels: none -> 76.5 us  [experts(): pl.pallas_call(moe_kernel, name='experts', out_shape=(jax.ShapeDtypeStruc...]
    psum x1 -> x0, blocking collectives: 65.8 us -> none  [on_device(): counts = lax.psum(local_counts, ('tp', 'ep'))]
    all_gather x2 -> x0, waiting for transfers between devices: 29.7 us -> none  [the longest x1 29.7 us: on_device(): arrived = lax.all_gather(landed[:, None], 'ep', axis=1, tiled=True)]
    dot_general x5 -> x0, matrix products: 22.9 us -> none  [the longest x1 10.1 us: on_device(): jnp.dot(active, w_down[0], preferred_element_type=jnp.float32)]
    all_to_all x1 -> x0, blocking collectives: 12.7 us -> none  [on_device(): lax.all_to_all(outgoing, 'tp', split_axis=0, concat_axis=0, tiled=True)]
    all_to_all x1 -> x0, waiting for transfers between devices: 9.24 us -> none  [on_device(): lax.all_to_all(outbound, 'tp', split_axis=0, concat_axis=0, tiled=True)]
    reshape x2 -> x1, local copies, waits for them, and re-layouts: 10.4 us -> 1.34 us  [experts(): norm_gain.reshape(1, -1)]
    all_gather x1 -> x0, local copies, waits for them, and re-layouts: 7.72 us -> none  [on_device(): arrived = lax.all_gather(landed[:, None], 'ep', axis=1, tiled=True)]
  transfers between devices with their start and end apart: 4 -> 0, of which waited for: 2 -> 0; matrix products, arithmetic and copies ran while one was open for 11% -> 0% of each run, Pallas kernels for 0% -> 0%
where the time goes in v2:
time: 230 us
  Pallas kernels  223 us (97%)
  local copies, waits for them, and re-layouts  5.85 us (3%)
    pallas_call x1, Pallas kernels, project(): pl.pallas_call(project_kernel, name='project', out_shape=jax.ShapeDtypeSt...  147 us
    pallas_call x1, Pallas kernels, experts(): pl.pallas_call(moe_kernel, name='experts', out_shape=(jax.ShapeDtypeStruc...  76.5 us

profile of v2, /device:TPU:1, one launch (start us, length us, event | category | flops | bytes accessed | tf_op | source)
XLA Modules:
  0.0 229.5 jit_solution(3552250769664512142)
XLA Ops:
  0.6 1.3 reshape.24.gain_ref
  2.0 146.5 %project.1.hid_ref = bf16[128,7168]{1,0:T(8,128)(2,1)} custom-call(bf16[4,4,128,512]{3,2,1,0:T(8,128)(2,1)} %bitcast.12, bf16[512,7168]{1,0:T(8,128)(2,1)} %w_ref.1, bf16[128,7168]{1,0:T(8,128)(2,1)} %res_ref.1), custom_call_target="tpu_custom_call" | custom-call | tf_op jit(solution)/shard_map/project/pallas_call | solution.py:229
  148.5 0.0 copy-start
  148.5 76.5 %experts.1 = (bf16[128,7168]{1,0:T(8,128)(2,1)}, f32[1,256]{1,0:T(1,128)}, f32[1,256]{1,0:T(1,128)}) custom-call(bf16[128,7168]{1,0:T(8,128)(2,1)} %project.1.hid_ref, bf16[1,7168]{1,0:T(2,128)(2,1)} %reshape.24.gain_ref, bf16[16,7168]{1,0:T(8,128)(2,1)} %bitcast.13, f32[1,256]{1,0:T(1,128)} %bitcast.17, s32[8,128]{1,0:T(8,128)} %bitcast.14, ...), custom_call_target="tpu_custom_call" | custom-call | tf_op jit(solution)/shard_map/experts/pallas_call | solution.py:546
  225.0 0.0 copy-start.1
  225.0 0.0 copy-done
  225.0 1.2 copy.18
  226.2 0.9 copy-done.1
  227.2 0.0 copy-start.3
  227.2 0.0 copy-start.2
  227.2 1.2 copy.19
  228.4 0.0 copy-done.3
  228.4 0.6 copy.20
  229.0 0.0 copy-done.2
  229.0 0.6 copy.21
Async XLA Ops:
  148.5 76.5 %copy-start = (bf16[128,7168]{1,0:T(8,128)(2,1)S(1)}, bf16[128,7168]{1,0:T(8,128)(2,1)}, u32[]{:S(2)}) copy-start(bf16[128,7168]{1,0:T(8,128)(2,1)} %project.1.hid_ref) | copy-start | bytes 5505028
  225.0 2.2 copy-start.1
  227.2 1.2 copy-start.3
  227.2 1.8 copy-start.2

commit v3 on v2

--- a/solution.py
+++ b/solution.py
@@ -16,6 +16,7 @@
 MESH = pl.DeviceIdType.MESH
 VMEM = pltpu.VMEM
 ROUNDS = 7
+SHARED = 6
 CH = 256
 
 
@@ -48,8 +49,8 @@
 
 def project_kernel(
     a_ref, w_ref, res_ref, out_ref,
-    ag, wown, wbuf, pbuf, rbuf, resv,
-    loc, a_s, a_r, y_s, y_r, x_s, x_r, f_s, f_r, c_s, c_r, z_s, z_r,
+    ag, wown, wbuf, pbuf, half_in, full_in, resv,
+    loc, a_s, a_r, y_s, y_r, g_s, g_r, v_s, v_r, x_s, x_r, f_s, f_r, c_s, c_r, h_s, h_r, z_s, z_r,
 ):
     z, y, x, c = place()
     half = pl.multiple_of(c * 256, 256)
@@ -69,16 +70,37 @@
     def chunk(dx, r):
         return ring(x + dx) * ROUNDS + r
 
-    def y_copy(r, e):
-        n = chunk(0, r)
+    def y_copy(i, n, way):
         cols = pl.ds(pl.multiple_of(n * CH, CH), CH)
         return remote(
-            w_ref.at[pl.ds(half, 256), cols], wbuf.at[n, 3 - e, pl.ds(half, 256), :],
-            y_s.at[r, e - 1], y_r.at[r, 3 - e], at(z, y + e, x, c),
+            w_ref.at[pl.ds(half, 256), cols], wbuf.at[n, 2 - 2 * way, pl.ds(half, 256), :],
+            y_s.at[i, way], y_r.at[i, way], at(z, y + 1 - 2 * way, x, c),
         )
 
-    def a_copy(e):
-        return remote(a_ref.at[:, ring(y + e)], ag.at[4 - e], a_s.at[e - 1], a_r.at[3 - e], at(z, y + e, x, c))
+    def y_land(i, n, way):
+        part = wbuf.at[n, 2 - 2 * way, pl.ds(half, 256), :]
+        return remote(part, part, y_s.at[i, way], y_r.at[i, way], at(z, y + 1, x, c))
+
+    def g_copy(i, n, way):
+        rows = pl.ds(pl.multiple_of(half + 128 * way, 128), 128)
+        return remote(
+            wbuf.at[n, 2 - 2 * way, rows, :], wbuf.at[n, 1, rows, :],
+            g_s.at[i, way], g_r.at[i, way], at(z, y + 1 - 2 * way, x, c),
+        )
+
+    def common(u):
+        return u * ROUNDS + SHARED
+
+    def v_copy(u):
+        part = wbuf.at[common(u), :, pl.ds(half, 256), :]
+        return remote(part, part, v_s.at[u], v_r.at[u], sib)
+
+    def v_land(u):
+        part = wbuf.at[common(u), :, pl.ds(pl.multiple_of(256 - half, 256), 256), :]
+        return remote(part, part, v_s.at[u], v_r.at[u], sib)
+
+    def a_copy(g, e):
+        return remote(a_ref.at[g, ring(y + e)], ag.at[4 - e, g], a_s.at[g, e - 1], a_r.at[g, 3 - e], at(z, y + e, x, c))
 
     def x_copy(r, way):
         part = wbuf.at[chunk(0, r), :, pl.ds(half, 256), :]
@@ -111,116 +133,204 @@
         part = wbuf.at[n, :, pl.ds(other, 256), :]
         return remote(part, part, c_s.at[r, q], c_r.at[r, q], sib)
 
-    def z_copy(n, e):
-        return remote(pbuf.at[n, ring(z + e)], rbuf.at[n, 3 - e], z_s.at[n, e - 1], z_r.at[n, 3 - e], at(z + e, y, x, c))
-
-    def z_land(n, k):
-        return remote(pbuf.at[n, 0], rbuf.at[n, k], z_s.at[n, k], z_r.at[n, k], at(z + 1, y, x, c))
-
-    def y_land(r, k):
-        n = chunk(0, r)
-        part = wbuf.at[n, k, pl.ds(half, 256), :]
-        return remote(part, part, y_s.at[r, k], y_r.at[r, k], at(z, y + 1, x, c))
-
-    def start_y(r):
-        for e in (1, 3, 2):
-            y_copy(r, e).start()
+    def halves(way):
+        return pl.ds(64 * way, 64)
+
+    def h_copy(n, way):
+        return remote(
+            pbuf.at[n, ring(z + 2), halves(way)], half_in.at[n, way],
+            h_s.at[n, way], h_r.at[n, way], at(z + 1 - 2 * way, y, x, c),
+        )
+
+    def z_copy(n, way):
+        to = z + 1 - 2 * way
+        return remote(pbuf.at[n, ring(to)], full_in.at[n, way], z_s.at[n, way], z_r.at[n, way], at(to, y, x, c))
+
+    def start_y(i, n):
+        for way in (0, 1):
+            y_copy(i, n, way).start()
+
+    def start_a(g):
+        for e in (2, 1, 3):
+            a_copy(g, e).start()
+
+    def pass_on(i, n):
+        for way in (0, 1):
+            y_land(i, n, way).wait_recv()
+            g_copy(i, n, way).start()
 
     def first(r):
-        for k in range(3):
-            y_land(r, k).wait_recv()
+        for way in (0, 1):
+            g_copy(r, chunk(0, r), way).wait_recv()
         x_copy(r, 0).start()
         x_copy(r, 1).start()
         c_copy(r, 0).start()
 
-        @pl.when(r + 2 < ROUNDS)
-        def _():
-            start_y(r + 2)
-
-    def multiply(r):
-        @pl.loop(0, 4)
-        def _(q):
-            dx = q + lax.div(q, 2) - 2 * lax.div(q, 3)
-            slot = q + lax.rem(q, 3) - 3 * lax.div(q, 2) + 3 * lax.div(q, 3)
-            n = chunk(dx, r)
-            c_land(n, r, slot).wait_recv()
-            cols = pl.ds(pl.multiple_of(n * CH, CH), CH)
-            total = jnp.dot(ag[0].reshape(512, 512), wown[:, cols], preferred_element_type=jnp.float32)
-            for k in range(3):
-                total += jnp.dot(ag[k + 1].reshape(512, 512), wbuf[n, k], preferred_element_type=jnp.float32)
-            pbuf[n] = total.astype(jnp.bfloat16).reshape(4, 128, CH)
-            for e in (2, 1, 3):
-                z_copy(n, e).start()
-
-    def finish(r):
-        @pl.loop(0, 4)
-        def _(q):
-            dx = q + lax.div(q, 2) - 2 * lax.div(q, 3)
-            n = chunk(dx, r)
-            for k in range(3):
-                z_land(n, k).wait_recv()
-            cols = pl.ds(pl.multiple_of(n * CH, CH), CH)
-            total = pbuf[n, z].astype(jnp.float32)
-            for k in range(3):
-                total += rbuf[n, k].astype(jnp.float32)
-            out_ref[:, cols] = (resv[:, cols].astype(jnp.float32) + total).astype(jnp.bfloat16)
-
-    start_y(0)
-    for e in (2, 1, 3):
-        a_copy(e).start()
-    start_y(1)
+    def multiply(n):
+        cols = pl.ds(pl.multiple_of(n * CH, CH), CH)
+        total = jnp.dot(ag[0].reshape(512, 512), wown[:, cols], preferred_element_type=jnp.float32)
+        for k in range(3):
+            total += jnp.dot(ag[k + 1].reshape(512, 512), wbuf[n, k], preferred_element_type=jnp.float32)
+        pbuf[n] = total.astype(jnp.bfloat16).reshape(4, 128, CH)
+        for way in (0, 1):
+            h_copy(n, way).start()
+
+    def combine(n):
+        for way in (0, 1):
+            to = ring(z + 1 - 2 * way)
+            h_copy(n, way).wait_recv()
+            both = pbuf[n, to, halves(way)].astype(jnp.float32) + half_in[n, way].astype(jnp.float32)
+            pbuf[n, to, halves(way)] = both.astype(jnp.bfloat16)
+            z_copy(n, way).start()
+
+    def finish(n):
+        cols = pl.ds(pl.multiple_of(n * CH, CH), CH)
+        total = pbuf[n, z].astype(jnp.float32)
+        for way in (0, 1):
+            z_copy(n, way).wait_recv()
+            total += full_in[n, way].astype(jnp.float32)
+        out_ref[:, cols] = (resv[:, cols].astype(jnp.float32) + total).astype(jnp.bfloat16)
+
+    def near(q, r):
+        return chunk(q + lax.div(q, 2), r)
+
+    def step(work, r):
+        @pl.when((r >= 0) & (r < SHARED))
+        def _():
+            @pl.loop(0, 3)
+            def _(q):
+                work(near(q, r))
+
+        @pl.when((r >= 3) & (r < 7))
+        def _():
+            work(common(r - 3))
+
+        @pl.when((r >= 1) & (r <= SHARED))
+        def _():
+            work(chunk(2, r - 1))
+
+    start_y(0, chunk(0, 0))
+    start_y(1, chunk(0, 1))
+    pass_on(0, chunk(0, 0))
+    start_a(0)
+    start_a(1)
+    pass_on(1, chunk(0, 1))
+    start_y(2, chunk(0, 2))
     first(0)
     first(1)
+    start_a(2)
+    start_a(3)
     own_a.wait()
     own_w.wait()
     own_res.wait()
 
-    @pl.loop(0, ROUNDS + 4)
+    def multiply_near(r):
+        @pl.loop(0, 3)
+        def _(q):
+            n = near(q, r)
+            c_land(n, r, lax.rem(3 - q, 3)).wait_recv()
+            multiply(n)
+
+    @pl.loop(0, SHARED + 4)
     def _(r):
-        @pl.when(r < ROUNDS)
+        @pl.when(r < SHARED)
         def _():
             for way in (0, 1):
                 x_land(r, way).wait_recv()
                 f_copy(r, way).start()
                 c_copy(r, 1 + way).start()
 
-        @pl.when(r + 2 < ROUNDS)
+        @pl.when(r + 2 < SHARED)
+        def _():
+            pass_on(r + 2, chunk(0, r + 2))
+
+        @pl.when(r + 3 < SHARED)
+        def _():
+            start_y(r + 3, chunk(0, r + 3))
+
+        @pl.when(r < 4)
+        def _():
+            start_y(SHARED + r, common(r))
+
+        @pl.when(r + 2 < SHARED)
         def _():
             first(r + 2)
 
+        @pl.when((r >= 1) & (r < 5))
+        def _():
+            pass_on(SHARED + r - 1, common(r - 1))
+
+        @pl.when((r >= 2) & (r < 6))
+        def _():
+            for way in (0, 1):
+                g_copy(SHARED + r - 2, common(r - 2), way).wait_recv()
+            v_copy(r - 2).start()
+
         @pl.when(r == 1)
         def _():
-            for k in range(3):
-                remote(ag.at[k + 1], ag.at[k + 1], a_s.at[k], a_r.at[k], at(z, y + 1, x, c)).wait_recv()
-
-        @pl.when((r >= 1) & (r <= ROUNDS))
+            for g in range(4):
+                for k in range(3):
+                    part = ag.at[k + 1, g]
+                    remote(part, part, a_s.at[g, k], a_r.at[g, k], at(z, y + 1, x, c)).wait_recv()
+            multiply_near(0)
+
+        @pl.when(r >= 2)
+        def _():
+            step(combine, r - 1)
+
+        @pl.when((r >= 1) & (r < SHARED))
+        def _():
+            multiply_near(r)
+
+        @pl.when((r >= 3) & (r < 7))
+        def _():
+            v_land(r - 3).wait_recv()
+            multiply(common(r - 3))
+
+        @pl.when((r >= 1) & (r <= SHARED))
         def _():
             for way in (0, 1):
                 f_land(r - 1, way).wait_recv()
             c_copy(r - 1, 3).start()
-            multiply(r - 1)
-
-        @pl.when(r >= 4)
-        def _():
-            finish(r - 4)
-
-    for e in (1, 2, 3):
-        a_copy(e).wait_send()
-
-    @pl.loop(0, ROUNDS)
+            c_land(chunk(2, r - 1), r - 1, 3).wait_recv()
+            multiply(chunk(2, r - 1))
+
+        @pl.when(r == 2)
+        def _():
+            @pl.loop(0, 3)
+            def _(q):
+                combine(near(q, 0))
+
+        @pl.when(r >= 3)
+        def _():
+            step(finish, r - 3)
+
+    for g in range(4):
+        for e in (1, 2, 3):
+            a_copy(g, e).wait_send()
+
+    @pl.loop(0, SHARED)
     def _(r):
-        for e in (1, 2, 3):
-            y_copy(r, e).wait_send()
-        for way in (0, 1):
+        for way in (0, 1):
+            y_copy(r, chunk(0, r), way).wait_send()
+            g_copy(r, chunk(0, r), way).wait_send()
             x_copy(r, way).wait_send()
             f_copy(r, way).wait_send()
         for q in range(4):
             c_copy(r, q).wait_send()
 
+    @pl.loop(0, 4)
+    def _(u):
+        for way in (0, 1):
+            y_copy(SHARED + u, common(u), way).wait_send()
+            g_copy(SHARED + u, common(u), way).wait_send()
+        v_copy(u).wait_send()
+
     @pl.loop(0, 4 * ROUNDS)
     def _(n):
-        for e in (1, 2, 3):
-            z_copy(n, e).wait_send()
+        for way in (0, 1):
+            h_copy(n, way).wait_send()
+            z_copy(n, way).wait_send()
 
 
 def project(attn_out, w_out, residual):
@@ -237,10 +347,12 @@
             VMEM((512, 7168), jnp.bfloat16),
             VMEM((28, 3, 512, CH), jnp.bfloat16),
             VMEM((28, 4, 128, CH), jnp.bfloat16),
-            VMEM((28, 3, 128, CH), jnp.bfloat16),
+            VMEM((28, 2, 64, CH), jnp.bfloat16),
+            VMEM((28, 2, 128, CH), jnp.bfloat16),
             VMEM((128, 7168), jnp.bfloat16),
-            dma((3,)), dma((3,)), dma((3,)), dma((7, 3)), dma((7, 3)), dma((7, 2)), dma((7, 2)),
-            dma((7, 2)), dma((7, 2)), dma((7, 4)), dma((7, 4)), dma((28, 3)), dma((28, 3)),
+            dma((3,)), dma((4, 3)), dma((4, 3)), dma((10, 2)), dma((10, 2)), dma((10, 2)), dma((10, 2)),
+            dma((4,)), dma((4,)), dma((6, 2)), dma((6, 2)), dma((6, 2)), dma((6, 2)), dma((6, 4)), dma((6, 4)),
+            dma((28, 2)), dma((28, 2)), dma((28, 2)), dma((28, 2)),
         ],
         compiler_params=pltpu.CompilerParams(
             collective_id=0, has_side_effects=True, vmem_limit_bytes=58 * 1024 * 1024

time: 230 us -> 207 us (0.900)
  Pallas kernels: 223 us -> 200 us
    pallas_call x1, Pallas kernels: 147 us -> 125 us  [project(): pl.pallas_call(project_kernel, name='project', out_shape=jax.ShapeDtypeSt...]
where the time goes in v3:
time: 207 us
  Pallas kernels  200 us (97%)
  local copies, waits for them, and re-layouts  5.85 us (3%)
    pallas_call x1, Pallas kernels, project(): pl.pallas_call(project_kernel, name='project', out_shape=jax.ShapeDtypeSt...  125 us
    pallas_call x1, Pallas kernels, experts(): pl.pallas_call(moe_kernel, name='experts', out_shape=(jax.ShapeDtypeStruc...  75.2 us
    unnamed x12, local copies, waits for them, and re-layouts  4.51 us

profile of v3, /device:TPU:1, one launch (start us, length us, event | category | flops | bytes accessed | tf_op | source)
XLA Modules:
  0.0 206.7 jit_solution(10479687375956872561)
XLA Ops:
  0.6 1.3 reshape.24.gain_ref
  2.0 125.0 %project.1.hid_ref = bf16[128,7168]{1,0:T(8,128)(2,1)} custom-call(bf16[4,4,128,512]{3,2,1,0:T(8,128)(2,1)} %bitcast.12, bf16[512,7168]{1,0:T(8,128)(2,1)} %w_ref.1, bf16[128,7168]{1,0:T(8,128)(2,1)} %res_ref.1), custom_call_target="tpu_custom_call" | custom-call | tf_op jit(solution)/shard_map/project/pallas_call | solution.py:339
  127.0 0.0 copy-start
  127.0 75.2 %experts.1 = (bf16[128,7168]{1,0:T(8,128)(2,1)}, f32[1,256]{1,0:T(1,128)}, f32[1,256]{1,0:T(1,128)}) custom-call(bf16[128,7168]{1,0:T(8,128)(2,1)} %project.1.hid_ref, bf16[1,7168]{1,0:T(2,128)(2,1)} %reshape.24.gain_ref, bf16[16,7168]{1,0:T(8,128)(2,1)} %bitcast.13, f32[1,256]{1,0:T(1,128)} %bitcast.17, s32[8,128]{1,0:T(8,128)} %bitcast.14, ...), custom_call_target="tpu_custom_call" | custom-call | tf_op jit(solution)/shard_map/experts/pallas_call | solution.py:658
  202.2 0.0 copy-start.1
  202.2 0.0 copy-done
  202.2 1.2 copy.18
  203.4 0.9 copy-done.1
  204.4 0.0 copy-start.3
  204.4 0.0 copy-start.2
  204.4 1.2 copy.19
  205.6 0.0 copy-done.3
  205.6 0.6 copy.20
  206.2 0.0 copy-done.2
  206.2 0.6 copy.21
Async XLA Ops:
  127.0 75.2 %copy-start = (bf16[128,7168]{1,0:T(8,128)(2,1)S(1)}, bf16[128,7168]{1,0:T(8,128)(2,1)}, u32[]{:S(2)}) copy-start(bf16[128,7168]{1,0:T(8,128)(2,1)} %project.1.hid_ref) | copy-start | bytes 5505028
  202.2 2.2 %copy-start.1 = (bf16[128,7168]{1,0:T(8,128)(2,1)S(1)}, bf16[128,7168]{1,0:T(8,128)(2,1)}, u32[]{:S(2)}) copy-start(bf16[128,7168]{1,0:T(8,128)(2,1)} %get-tuple-element.15) | copy-start | bytes 5505028
  204.4 1.2 copy-start.3
  204.4 1.8 copy-start.2

commit v4 on v3

--- a/solution.py
+++ b/solution.py
@@ -367,9 +367,9 @@
 def moe_kernel(
     hid_ref, gain_ref, rout_ref, bias_ref, cho_ref, wg_ref, wu_ref, wd_ref,
     moe_ref, load_ref, next_ref,
-    wg, wu, wd, rt, normed, snd, land, rows, ybuf, r1, sbuf, r2, rsend, ret, cnt, cnt_tp, cnt_ep,
-    loc, d_s, d_r, ax_s, ax_r, ac_s, ac_r, k_s, k_r, l_s, l_r, rt_s, rt_r, rs_s, rs_r,
-    p_s, p_r, q_s, q_r, b_s, b_r,
+    wg, wu, wd, rt, normed, gain, snd, land, rows, ybuf, r1, sbuf, half_in, full_in, rsend, ret, cnt, cnt_tp, cnt_ep,
+    loc, d_s, d_r, ax_s, ax_r, af_s, af_r, ac_s, ac_r, k_s, k_r, l_s, l_r, rt_s, rt_r, rs_s, rs_r,
+    p_s, p_r, h_s, h_r, q_s, q_r, b_s, b_r,
 ):
     z, y, x, c = place()
     tp = z * 4 + y
@@ -397,15 +397,6 @@
 
     def cut(j):
         return slice(j * LANE, (j + 1) * LANE)
-
-    ssq = jnp.zeros((128, 1), jnp.float32)
-    for j in range(8):
-        h = hid_ref[:, cut(j)].astype(jnp.float32)
-        ssq += jnp.sum(h * h, axis=1, keepdims=True)
-    scale = lax.rsqrt(ssq / width + norm_eps)
-    for j in range(8):
-        h = hid_ref[:, cut(j)].astype(jnp.float32)
-        normed[:, cut(j)] = (h * scale * gain_ref[:, cut(j)].astype(jnp.float32)).astype(jnp.bfloat16)
 
     row = lax.broadcasted_iota(jnp.int32, (256, 128), 0)
     lane = lax.broadcasted_iota(jnp.int32, (256, 128), 1)
@@ -421,10 +412,17 @@
     slot = ((row // 8) % 2).astype(jnp.float32)
     pick = jnp.where(rank == slot, member, 0.0)
     feature = row % 8
-    outgoing = jnp.zeros((256, LANE), jnp.float32)
+    picked = jnp.zeros((256, LANE), jnp.float32)
     for j in range(8):
         pj = jnp.where(feature == j, pick, 0.0).astype(jnp.bfloat16)
-        outgoing += jnp.dot(pj, normed[:, cut(j)], preferred_element_type=jnp.float32)
+        picked += jnp.dot(pj, hid_ref[:, cut(j)], preferred_element_type=jnp.float32)
+    gains = gain_ref[...].astype(jnp.float32)
+    for j in range(8):
+        for i in range(7):
+            gain[j : j + 1, i * 128 : (i + 1) * 128] = gains[j * 7 + i : j * 7 + i + 1, :]
+    picked = picked.reshape(32, 8, LANE)
+    ssq = jnp.sum(jnp.sum(picked * picked, axis=2, keepdims=True), axis=1, keepdims=True)
+    outgoing = picked * lax.rsqrt(ssq / width + norm_eps) * gain[...][None]
     snd[...] = outgoing.astype(jnp.bfloat16).reshape(16, 16, LANE)
     contract_last = (((1,), (1,)), ((), ()))
     cnt[...] = lax.dot_general(
@@ -451,13 +449,24 @@
     def group(dz):
         return pl.ds(pl.multiple_of(ring(z + dz) * 4, 4), 4)
 
-    def x_copy(g, dz, e):
+    def x_copy(g, dz, way):
         part = land.at[ep, group(dz)]
-        return remote(part, part, ax_s.at[g, e - 1], ax_r.at[g, 3 - e], (tp, ep_at(e, 0)))
-
-    def x_land(g, dz, k):
-        part = land.at[ep_at(k + 1, 0), group(dz)]
-        return remote(part, part, ax_s.at[g, k], ax_r.at[g, k], (tp, ep_at(1, 0)))
+        return remote(part, part, ax_s.at[g, way], ax_r.at[g, way], (tp, ep_at(1 - 2 * way, 0)))
+
+    def x_land(g, dz, way):
+        part = land.at[ep_at(2 * way - 1, 0), group(dz)]
+        return remote(part, part, ax_s.at[g, way], ax_r.at[g, way], (tp, ep_at(1, 0)))
+
+    def f_rows(dx, dz, way):
+        return land.at[ep_at(dx, 0), pl.ds(pl.multiple_of(ring(z + dz) * 4 + 2 * way, 2), 2)]
+
+    def f_copy(g, dz, way):
+        part = f_rows(2 * way - 1, dz, way)
+        return remote(part, part, af_s.at[g, way], af_r.at[g, way], (tp, ep_at(1 - 2 * way, 0)))
+
+    def f_land(g, dz, way):
+        part = f_rows(2, dz, way)
+        return remote(part, part, af_s.at[g, way], af_r.at[g, way], (tp, ep_at(1, 0)))
 
     def c_copy(g, dz, q):
         part = land.at[ep_at(q, 0), group(dz)]
@@ -477,8 +486,8 @@
                 d_land(p).wait_recv()
         if dz == 0:
             own_rows.wait()
-        for e in (1, 3, 2):
-            x_copy(g, dz, e).start()
+        for way in (0, 1):
+            x_copy(g, dz, way).start()
         c_copy(g, dz, 0).start()
 
     def rt_copy(p):
@@ -506,24 +515,39 @@
     for p in ep_peers:
         l_copy(p).start()
 
-    for g, dz in GROUPS:
-        for k in (0, 2, 1):
-            x_land(g, dz, k).wait_recv()
-            c_copy(g, dz, k + 1).start()
-    for g, dz in GROUPS:
-        for q in range(4):
-            c_land(g, dz, q).wait_recv()
     out_row = lax.broadcasted_iota(jnp.int32, (128, 128), 0)
     in_row = lax.broadcasted_iota(jnp.int32, (128, 128), 1)
     source = ((out_row % 16) // 2) * 16 + (out_row % 2) * 8 + out_row // 16
     perm = jnp.where(in_row == source, 1.0, 0.0).astype(jnp.bfloat16)
 
-    @pl.loop(0, 16)
-    def _(i):
-        group_of, part = lax.div(i, 2), lax.rem(i, 2)
-        block = land[group_of, pl.ds(pl.multiple_of(part * 8, 8), 8)].reshape(128, LANE)
-        turned = jnp.dot(perm, block, preferred_element_type=jnp.float32).astype(jnp.bfloat16)
-        rows[:, pl.ds(pl.multiple_of(i * 16, 16), 16), :] = turned.reshape(8, 16, LANE)
+    def turn_rows(group_of):
+        for part in range(2):
+            block = land[group_of, part * 8 : part * 8 + 8].reshape(128, LANE)
+            turned = jnp.dot(perm, block, preferred_element_type=jnp.float32).astype(jnp.bfloat16)
+            to = pl.ds(pl.multiple_of(group_of * 32 + part * 16, 16), 16)
+            rows[:, to, :] = turned.reshape(8, 16, LANE)
+
+    turn_rows(ep)
+    for g, dz in GROUPS:
+        for way in (0, 1):
+            x_land(g, dz, way).wait_recv()
+            f_copy(g, dz, way).start()
+            c_copy(g, dz, 3 - 2 * way).start()
+    for q in (0, 3, 1):
+        if q:
+            turn_rows(ep_at(q, 0))
+        if q == 1:
+            for g, dz in GROUPS:
+                for way in (0, 1):
+                    f_land(g, dz, way).wait_recv()
+                c_copy(g, dz, 2).start()
+        for g, dz in GROUPS:
+            c_land(g, dz, q).wait_recv()
+        turn_rows(ep_at(q, 1))
+    turn_rows(ep_at(2, 0))
+    for g, dz in GROUPS:
+        c_land(g, dz, 2).wait_recv()
+    turn_rows(ep_at(2, 1))
 
     for load in loads:
         load.wait()
@@ -537,11 +561,27 @@
     def p_copy(n):
         return remote(ybuf.at[n, :, 1 - c], r1.at[n], p_s.at[n], p_r.at[n], sib)
 
-    def q_copy(n, e):
-        return remote(sbuf.at[n, ring(x + e)], r2.at[n, 3 - e], q_s.at[n, e - 1], q_r.at[n, 3 - e], (tp, ep_at(e, 0)))
-
-    def q_land(n, k):
-        return remote(r2.at[n, k], r2.at[n, k], q_s.at[n, k], q_r.at[n, k], (tp, ep_at(1, 0)))
+    def h_copy(n, way):
+        rows_of = pl.ds(16 * way, 16)
+        return remote(
+            sbuf.at[n, ring(x + 2), rows_of], half_in.at[n, way],
+            h_s.at[n, way], h_r.at[n, way], (tp, ep_at(1 - 2 * way, 0)),
+        )
+
+    def q_copy(n, way):
+        to = 1 - 2 * way
+        return remote(
+            sbuf.at[n, ring(x + to)], full_in.at[n, way], q_s.at[n, way], q_r.at[n, way], (tp, ep_at(to, 0))
+        )
+
+    def forward(n):
+        for way in (0, 1):
+            to = ring(x + 1 - 2 * way)
+            h_copy(n, way).wait_recv()
+            rows_of = slice(16 * way, 16 * way + 16)
+            both = sbuf[n, to, rows_of].astype(jnp.float32) + half_in[n, way].astype(jnp.float32)
+            sbuf[n, to, rows_of] = both.astype(jnp.bfloat16)
+            q_copy(n, way).start()
 
     for n in range(4):
         part = jnp.dot(active, wd[:, n * 2 * LANE : (n + 1) * 2 * LANE], preferred_element_type=jnp.float32)
@@ -552,8 +592,11 @@
         for i in range(4):
             both = ybuf[n, i, c].astype(jnp.float32) + r1[n, i].astype(jnp.float32)
             sbuf[n, i] = both.astype(jnp.bfloat16)
-        for e in (1, 3, 2):
-            q_copy(n, e).start()
+        for way in (0, 1):
+            h_copy(n, way).start()
+        if n:
+            forward(n - 1)
+    forward(3)
 
     for p in ep_peers:
         peer = ep_at(*p)
@@ -576,6 +619,14 @@
     rt_sib = remote(mine, mine, rs_s.at[0], rs_r.at[0], sib)
     rt_sib.start()
     other = rt.at[:, :, pl.ds(pl.multiple_of((1 - c) * (width // 2), width // 2), width // 2)]
+    ssq = jnp.zeros((128, 1), jnp.float32)
+    for j in range(8):
+        h = hid_ref[:, cut(j)].astype(jnp.float32)
+        ssq += jnp.sum(h * h, axis=1, keepdims=True)
+    scale = lax.rsqrt(ssq / width + norm_eps)
+    for j in range(8):
+        h = hid_ref[:, cut(j)].astype(jnp.float32)
+        normed[:, cut(j)] = (h * scale * gain[j : j + 1, :]).astype(jnp.bfloat16)
     remote(other, other, rs_s.at[0], rs_r.at[0], sib).wait_recv()
     logits = jnp.zeros((256, 128), jnp.float32)
     for j in range(8):
@@ -600,11 +651,10 @@
     back_col = lax.broadcasted_iota(jnp.int32, (256, 32), 1)
     returned = jnp.zeros((256, LANE), jnp.float32)
     for n in range(4):
-        for k in (0, 2, 1):
-            q_land(n, k).wait_recv()
         total = sbuf[n, x].astype(jnp.float32)
-        for k in range(3):
-            total += r2[n, k].astype(jnp.float32)
+        for way in (0, 1):
+            q_copy(n, way).wait_recv()
+            total += full_in[n, way].astype(jnp.float32)
         total = total.astype(jnp.bfloat16)
         for i in range(2):
             turn = jnp.where((back_row // 8 == back_col) & (back_row % 8 == 2 * n + i), 1.0, 0.0).astype(jnp.bfloat16)
@@ -640,14 +690,16 @@
         l_copy(p).wait_send()
     rt_sib.wait_send()
     for g, dz in GROUPS:
-        for e in (1, 2, 3):
-            x_copy(g, dz, e).wait_send()
+        for way in (0, 1):
+            x_copy(g, dz, way).wait_send()
+            f_copy(g, dz, way).wait_send()
         for q in range(4):
             c_copy(g, dz, q).wait_send()
     for n in range(4):
         p_copy(n).wait_send()
-        for e in (1, 2, 3):
-            q_copy(n, e).wait_send()
+        for way in (0, 1):
+            h_copy(n, way).wait_send()
+            q_copy(n, way).wait_send()
 
 
 def experts(hidden_out, norm_gain, router, router_bias, choices, w_gate, w_up, w_down):
@@ -667,21 +719,21 @@
         out_specs=(vmem,) * 3,
         scratch_shapes=[
             VMEM((7168, 256), bf16), VMEM((7168, 256), bf16), VMEM((256, 7168), bf16),
-            VMEM((16, 16, 7168), bf16), VMEM((128, 7168), bf16), VMEM((16, 16, LANE), bf16),
+            VMEM((16, 16, 7168), bf16), VMEM((128, 7168), bf16), VMEM((8, LANE), f32), VMEM((16, 16, LANE), bf16),
             VMEM((8, 16, 16, LANE), bf16), VMEM((8, 256, LANE), bf16),
             VMEM((4, 4, 2, 32, 2 * LANE), bf16), VMEM((4, 4, 32, 2 * LANE), bf16),
-            VMEM((4, 4, 32, 2 * LANE), bf16), VMEM((4, 3, 32, 2 * LANE), bf16),
+            VMEM((4, 4, 32, 2 * LANE), bf16), VMEM((4, 2, 16, 2 * LANE), bf16), VMEM((4, 2, 32, 2 * LANE), bf16),
             VMEM((16, 16, LANE), bf16), VMEM((16, 16, LANE), bf16),
             VMEM((8, 256), f32), VMEM((16, 8, 256), f32), VMEM((8, 8, 256), f32),
-            dma((6,)), dma((16,)), dma((16,)), dma((4, 3)), dma((4, 3)), dma((4, 4)), dma((4, 4)),
+            dma((6,)), dma((16,)), dma((16,)), dma((4, 2)), dma((4, 2)), dma((4, 2)), dma((4, 2)), dma((4, 4)), dma((4, 4)),
             dma((16,)), dma((16,)), dma((8,)), dma((8,)), dma((16,)), dma((16,)), dma((1,)), dma((1,)),
-            dma((4,)), dma((4,)), dma((4, 3)), dma((4, 3)), dma((16,)), dma((16,)),
+            dma((4,)), dma((4,)), dma((4, 2)), dma((4, 2)), dma((4, 2)), dma((4, 2)), dma((16,)), dma((16,)),
         ],
         compiler_params=pltpu.CompilerParams(
             collective_id=1, has_side_effects=True, vmem_limit_bytes=56 * 1024 * 1024
         ),
     )(
-        hidden_out, norm_gain.reshape(1, -1), router.T, router_bias.reshape(1, -1), choices.T,
+        hidden_out, norm_gain.reshape(-1, 128), router.T, router_bias.reshape(1, -1), choices.T,
         w_gate[0], w_up[0], w_down[0],
     )
     return moe_out, load.reshape(-1), bias_next.reshape(-1)

time: 207 us -> 197 us (0.952)
  Pallas kernels: 200 us -> 192 us
    pallas_call x1, Pallas kernels: 75.2 us -> 67.1 us  [experts(): pl.pallas_call(moe_kernel, name='experts', out_shape=(jax.ShapeDtypeStruc...]
where the time goes in v4:
time: 197 us
  Pallas kernels  192 us (97%)
  local copies, waits for them, and re-layouts  4.51 us (2%)
    pallas_call x1, Pallas kernels, project(): pl.pallas_call(project_kernel, name='project', out_shape=jax.ShapeDtypeSt...  125 us
    pallas_call x1, Pallas kernels, experts(): pl.pallas_call(moe_kernel, name='experts', out_shape=(jax.ShapeDtypeStruc...  67.1 us
    unnamed x12, local copies, waits for them, and re-layouts  4.51 us

profile of v4, /device:TPU:1, one launch (start us, length us, event | category | flops | bytes accessed | tf_op | source)
XLA Modules:
  0.0 197.2 jit_solution(2468414590870551842)
XLA Ops:
  0.6 124.9 %project.1.hid_ref = bf16[128,7168]{1,0:T(8,128)(2,1)} custom-call(bf16[4,4,128,512]{3,2,1,0:T(8,128)(2,1)} %bitcast.13, bf16[512,7168]{1,0:T(8,128)(2,1)} %w_ref.1, bf16[128,7168]{1,0:T(8,128)(2,1)} %res_ref.1), custom_call_target="tpu_custom_call" | custom-call | tf_op jit(solution)/shard_map/project/pallas_call | solution.py:339
  125.6 0.0 copy-start
  125.6 67.1 %experts.1 = (bf16[128,7168]{1,0:T(8,128)(2,1)}, f32[1,256]{1,0:T(1,128)}, f32[1,256]{1,0:T(1,128)}) custom-call(bf16[128,7168]{1,0:T(8,128)(2,1)} %project.1.hid_ref, bf16[56,128]{1,0:T(8,128)(2,1)} %bitcast.15, bf16[16,7168]{1,0:T(8,128)(2,1)} %bitcast.14, f32[1,256]{1,0:T(1,128)} %bitcast.17, s32[8,128]{1,0:T(8,128)} %bitcast.16, ...), custom_call_target="tpu_custom_call" | custom-call | tf_op jit(solution)/shard_map/experts/pallas_call | solution.py:710
  192.6 0.0 copy-start.1
  192.7 0.0 copy-done
  192.7 1.2 copy.18
  193.9 0.9 copy-done.1
  194.8 0.0 copy-start.3
  194.8 0.0 copy-start.2
  194.8 1.2 copy.19
  196.0 0.0 copy-done.3
  196.0 0.6 copy.20
  196.6 0.0 copy-done.2
  196.6 0.6 copy.21
Async XLA Ops:
  125.6 67.1 %copy-start = (bf16[128,7168]{1,0:T(8,128)(2,1)S(1)}, bf16[128,7168]{1,0:T(8,128)(2,1)}, u32[]{:S(2)}) copy-start(bf16[128,7168]{1,0:T(8,128)(2,1)} %project.1.hid_ref) | copy-start | bytes 5505028
  192.6 2.2 %copy-start.1 = (bf16[128,7168]{1,0:T(8,128)(2,1)S(1)}, bf16[128,7168]{1,0:T(8,128)(2,1)}, u32[]{:S(2)}) copy-start(bf16[128,7168]{1,0:T(8,128)(2,1)} %get-tuple-element.15) | copy-start | bytes 5505028
  194.8 1.2 copy-start.3
  194.8 1.8 copy-start.2

commit v5 on v4

--- a/solution.py
+++ b/solution.py
@@ -54,10 +54,12 @@
 ):
     z, y, x, c = place()
     half = pl.multiple_of(c * 256, 256)
-    own_a = pltpu.make_async_copy(a_ref.at[:, y], ag.at[0], loc.at[0])
+    own_a = pltpu.make_async_copy(a_ref.at[:, y], ag.at[0, 0], loc.at[0])
+    own_b = pltpu.make_async_copy(a_ref.at[z], ag.at[1, 0], loc.at[3])
     own_w = pltpu.make_async_copy(w_ref, wown, loc.at[1])
     own_res = pltpu.make_async_copy(res_ref, resv, loc.at[2])
     own_a.start()
+    own_b.start()
     own_w.start()
     own_res.start()
     greet(
@@ -67,6 +69,15 @@
     )
     sib = at(z, y, x, c + 1)
 
+    def gather_at(kind, i):
+        return at(z + i * kind, y + i * (1 - kind), x, c)
+
+    def sum_at(kind, i):
+        return at(z + i * (1 - kind), y + i * kind, x, c)
+
+    def sum_place(kind):
+        return z * (1 - kind) + y * kind
+
     def chunk(dx, r):
         return ring(x + dx) * ROUNDS + r
 
@@ -74,7 +85,7 @@
         cols = pl.ds(pl.multiple_of(n * CH, CH), CH)
         return remote(
             w_ref.at[pl.ds(half, 256), cols], wbuf.at[n, 2 - 2 * way, pl.ds(half, 256), :],
-            y_s.at[i, way], y_r.at[i, way], at(z, y + 1 - 2 * way, x, c),
+            y_s.at[i, way], y_r.at[i, way], gather_at(lax.rem(i, 2), 1 - 2 * way),
         )
 
     def y_land(i, n, way):
@@ -85,7 +96,7 @@
         rows = pl.ds(pl.multiple_of(half + 128 * way, 128), 128)
         return remote(
             wbuf.at[n, 2 - 2 * way, rows, :], wbuf.at[n, 1, rows, :],
-            g_s.at[i, way], g_r.at[i, way], at(z, y + 1 - 2 * way, x, c),
+            g_s.at[i, way], g_r.at[i, way], gather_at(lax.rem(i, 2), 1 - 2 * way),
         )
 
     def common(u):
@@ -99,8 +110,11 @@
         part = wbuf.at[common(u), :, pl.ds(pl.multiple_of(256 - half, 256), 256), :]
         return remote(part, part, v_s.at[u], v_r.at[u], sib)
 
-    def a_copy(g, e):
-        return remote(a_ref.at[g, ring(y + e)], ag.at[4 - e, g], a_s.at[g, e - 1], a_r.at[g, 3 - e], at(z, y + e, x, c))
+    def a_copy(kind, g, e):
+        rows = a_ref.at[ring(z + e), g] if kind else a_ref.at[g, ring(y + e)]
+        return remote(
+            rows, ag.at[kind, 4 - e, g], a_s.at[kind, g, e - 1], a_r.at[kind, g, 3 - e], gather_at(kind, e)
+        )
 
     def x_copy(r, way):
         part = wbuf.at[chunk(0, r), :, pl.ds(half, 256), :]
@@ -136,15 +150,17 @@
     def halves(way):
         return pl.ds(64 * way, 64)
 
-    def h_copy(n, way):
+    def h_copy(n, kind, way):
         return remote(
-            pbuf.at[n, ring(z + 2), halves(way)], half_in.at[n, way],
-            h_s.at[n, way], h_r.at[n, way], at(z + 1 - 2 * way, y, x, c),
+            pbuf.at[n, ring(sum_place(kind) + 2), halves(way)], half_in.at[n, way],
+            h_s.at[n, way], h_r.at[n, way], sum_at(kind, 1 - 2 * way),
         )
 
-    def z_copy(n, way):
-        to = z + 1 - 2 * way
-        return remote(pbuf.at[n, ring(to)], full_in.at[n, way], z_s.at[n, way], z_r.at[n, way], at(to, y, x, c))
+    def z_copy(n, kind, way):
+        return remote(
+            pbuf.at[n, ring(sum_place(kind) + 1 - 2 * way)], full_in.at[n, way],
+            z_s.at[n, way], z_r.at[n, way], sum_at(kind, 1 - 2 * way),
+        )
 
     def start_y(i, n):
         for way in (0, 1):
@@ -152,7 +168,8 @@
 
     def start_a(g):
         for e in (2, 1, 3):
-            a_copy(g, e).start()
+            for kind in (0, 1):
+                a_copy(kind, g, e).start()
 
     def pass_on(i, n):
         for way in (0, 1):
@@ -166,28 +183,28 @@
         x_copy(r, 1).start()
         c_copy(r, 0).start()
 
-    def multiply(n):
+    def multiply(n, kind):
         cols = pl.ds(pl.multiple_of(n * CH, CH), CH)
-        total = jnp.dot(ag[0].reshape(512, 512), wown[:, cols], preferred_element_type=jnp.float32)
+        total = jnp.dot(ag[kind, 0].reshape(512, 512), wown[:, cols], preferred_element_type=jnp.float32)
         for k in range(3):
-            total += jnp.dot(ag[k + 1].reshape(512, 512), wbuf[n, k], preferred_element_type=jnp.float32)
+            total += jnp.dot(ag[kind, k + 1].reshape(512, 512), wbuf[n, k], preferred_element_type=jnp.float32)
         pbuf[n] = total.astype(jnp.bfloat16).reshape(4, 128, CH)
         for way in (0, 1):
-            h_copy(n, way).start()
-
-    def combine(n):
-        for way in (0, 1):
-            to = ring(z + 1 - 2 * way)
-            h_copy(n, way).wait_recv()
+            h_copy(n, kind, way).start()
+
+    def combine(n, kind):
+        for way in (0, 1):
+            to = ring(sum_place(kind) + 1 - 2 * way)
+            h_copy(n, kind, way).wait_recv()
             both = pbuf[n, to, halves(way)].astype(jnp.float32) + half_in[n, way].astype(jnp.float32)
             pbuf[n, to, halves(way)] = both.astype(jnp.bfloat16)
-            z_copy(n, way).start()
-
-    def finish(n):
+            z_copy(n, kind, way).start()
+
+    def finish(n, kind):
         cols = pl.ds(pl.multiple_of(n * CH, CH), CH)
-        total = pbuf[n, z].astype(jnp.float32)
-        for way in (0, 1):
-            z_copy(n, way).wait_recv()
+        total = pbuf[n, sum_place(kind)].astype(jnp.float32)
+        for way in (0, 1):
+            z_copy(n, kind, way).wait_recv()
             total += full_in[n, way].astype(jnp.float32)
         out_ref[:, cols] = (resv[:, cols].astype(jnp.float32) + total).astype(jnp.bfloat16)
 
@@ -199,28 +216,30 @@
         def _():
             @pl.loop(0, 3)
             def _(q):
-                work(near(q, r))
+                work(near(q, r), lax.rem(r, 2))
 
         @pl.when((r >= 3) & (r < 7))
         def _():
-            work(common(r - 3))
+            work(common(r - 3), lax.rem(r - 3, 2))
 
         @pl.when((r >= 1) & (r <= SHARED))
         def _():
-            work(chunk(2, r - 1))
+            work(chunk(2, r - 1), lax.rem(r - 1, 2))
 
     start_y(0, chunk(0, 0))
     start_y(1, chunk(0, 1))
     pass_on(0, chunk(0, 0))
+    pass_on(1, chunk(0, 1))
     start_a(0)
     start_a(1)
-    pass_on(1, chunk(0, 1))
-    start_y(2, chunk(0, 2))
     first(0)
     first(1)
     start_a(2)
+    start_y(2, chunk(0, 2))
+    start_y(3, chunk(0, 3))
     start_a(3)
     own_a.wait()
+    own_b.wait()
     own_w.wait()
     own_res.wait()
 
@@ -229,7 +248,7 @@
         def _(q):
             n = near(q, r)
             c_land(n, r, lax.rem(3 - q, 3)).wait_recv()
-            multiply(n)
+            multiply(n, lax.rem(r, 2))
 
     @pl.loop(0, SHARED + 4)
     def _(r):
@@ -244,7 +263,7 @@
         def _():
             pass_on(r + 2, chunk(0, r + 2))
 
-        @pl.when(r + 3 < SHARED)
+        @pl.when((r >= 1) & (r + 3 < SHARED))
         def _():
             start_y(r + 3, chunk(0, r + 3))
 
@@ -270,8 +289,9 @@
         def _():
             for g in range(4):
                 for k in range(3):
-                    part = ag.at[k + 1, g]
-                    remote(part, part, a_s.at[g, k], a_r.at[g, k], at(z, y + 1, x, c)).wait_recv()
+                    for kind in (0, 1):
+                        part = ag.at[kind, k + 1, g]
+                        remote(part, part, a_s.at[kind, g, k], a_r.at[kind, g, k], at(z, y + 1, x, c)).wait_recv()
             multiply_near(0)
 
         @pl.when(r >= 2)
@@ -285,7 +305,7 @@
         @pl.when((r >= 3) & (r < 7))
         def _():
             v_land(r - 3).wait_recv()
-            multiply(common(r - 3))
+            multiply(common(r - 3), lax.rem(r - 3, 2))
 
         @pl.when((r >= 1) & (r <= SHARED))
         def _():
@@ -293,13 +313,13 @@
                 f_land(r - 1, way).wait_recv()
             c_copy(r - 1, 3).start()
             c_land(chunk(2, r - 1), r - 1, 3).wait_recv()
-            multiply(chunk(2, r - 1))
+            multiply(chunk(2, r - 1), lax.rem(r - 1, 2))
 
         @pl.when(r == 2)
         def _():
             @pl.loop(0, 3)
             def _(q):
-                combine(near(q, 0))
+                combine(near(q, 0), 0)
 
         @pl.when(r >= 3)
         def _():
@@ -307,7 +327,8 @@
 
     for g in range(4):
         for e in (1, 2, 3):
-            a_copy(g, e).wait_send()
+            for kind in (0, 1):
+                a_copy(kind, g, e).wait_send()
 
     @pl.loop(0, SHARED)
     def _(r):
@@ -329,8 +350,8 @@
     @pl.loop(0, 4 * ROUNDS)
     def _(n):
         for way in (0, 1):
-            h_copy(n, way).wait_send()
-            z_copy(n, way).wait_send()
+            h_copy(n, 0, way).wait_send()
+            z_copy(n, 0, way).wait_send()
 
 
 def project(attn_out, w_out, residual):
@@ -343,14 +364,14 @@
         in_specs=[anywhere] * 3,
         out_specs=pl.BlockSpec(memory_space=VMEM),
         scratch_shapes=[
-            VMEM((4, 4, 128, 512), jnp.bfloat16),
+            VMEM((2, 4, 4, 128, 512), jnp.bfloat16),
             VMEM((512, 7168), jnp.bfloat16),
             VMEM((28, 3, 512, CH), jnp.bfloat16),
             VMEM((28, 4, 128, CH), jnp.bfloat16),
             VMEM((28, 2, 64, CH), jnp.bfloat16),
             VMEM((28, 2, 128, CH), jnp.bfloat16),
             VMEM((128, 7168), jnp.bfloat16),
-            dma((3,)), dma((4, 3)), dma((4, 3)), dma((10, 2)), dma((10, 2)), dma((10, 2)), dma((10, 2)),
+            dma((4,)), dma((2, 4, 3)), dma((2, 4, 3)), dma((10, 2)), dma((10, 2)), dma((10, 2)), dma((10, 2)),
             dma((4,)), dma((4,)), dma((6, 2)), dma((6, 2)), dma((6, 2)), dma((6, 2)), dma((6, 4)), dma((6, 4)),
             dma((28, 2)), dma((28, 2)), dma((28, 2)), dma((28, 2)),
         ],

time: 197 us -> 189 us (0.959)
  Pallas kernels: 192 us -> 183 us
    pallas_call x1, Pallas kernels: 125 us -> 118 us  [project(): pl.pallas_call(project_kernel, name='project', out_shape=jax.ShapeDtypeSt...]
where the time goes in v5:
time: 189 us; the launch traced here: 188 us
  Pallas kernels  183 us (97%)
  local copies, waits for them, and re-layouts  4.51 us (2%)
    pallas_call x1, Pallas kernels, project(): pl.pallas_call(project_kernel, name='project', out_shape=jax.ShapeDtypeSt...  118 us
    pallas_call x1, Pallas kernels, experts(): pl.pallas_call(moe_kernel, name='experts', out_shape=(jax.ShapeDtypeStruc...  65.1 us
    unnamed x12, local copies, waits for them, and re-layouts  4.51 us

profile of v5, /device:TPU:1, one launch (start us, length us, event | category | flops | bytes accessed | tf_op | source)
XLA Modules:
  0.0 188.4 jit_solution(794354892601160556)
XLA Ops:
  0.6 118.0 %project.1.hid_ref = bf16[128,7168]{1,0:T(8,128)(2,1)} custom-call(bf16[4,4,128,512]{3,2,1,0:T(8,128)(2,1)} %bitcast.13, bf16[512,7168]{1,0:T(8,128)(2,1)} %w_ref.1, bf16[128,7168]{1,0:T(8,128)(2,1)} %res_ref.1), custom_call_target="tpu_custom_call" | custom-call | tf_op jit(solution)/shard_map/project/pallas_call | solution.py:360
  118.7 0.0 copy-start
  118.7 65.1 %experts.1 = (bf16[128,7168]{1,0:T(8,128)(2,1)}, f32[1,256]{1,0:T(1,128)}, f32[1,256]{1,0:T(1,128)}) custom-call(bf16[128,7168]{1,0:T(8,128)(2,1)} %project.1.hid_ref, bf16[56,128]{1,0:T(8,128)(2,1)} %bitcast.15, bf16[16,7168]{1,0:T(8,128)(2,1)} %bitcast.14, f32[1,256]{1,0:T(1,128)} %bitcast.17, s32[8,128]{1,0:T(8,128)} %bitcast.16, ...), custom_call_target="tpu_custom_call" | custom-call | tf_op jit(solution)/shard_map/experts/pallas_call | solution.py:731
  183.8 0.0 copy-start.1
  183.9 0.0 copy-done
  183.9 1.2 copy.18
  185.1 0.9 copy-done.1
  186.0 0.0 copy-start.3
  186.0 0.0 copy-start.2
  186.0 1.2 copy.19
  187.2 0.0 copy-done.3
  187.2 0.6 copy.20
  187.8 0.0 copy-done.2
  187.8 0.6 copy.21
Async XLA Ops:
  118.7 65.2 %copy-start = (bf16[128,7168]{1,0:T(8,128)(2,1)S(1)}, bf16[128,7168]{1,0:T(8,128)(2,1)}, u32[]{:S(2)}) copy-start(bf16[128,7168]{1,0:T(8,128)(2,1)} %project.1.hid_ref) | copy-start | bytes 5505028
  183.8 2.2 %copy-start.1 = (bf16[128,7168]{1,0:T(8,128)(2,1)S(1)}, bf16[128,7168]{1,0:T(8,128)(2,1)}, u32[]{:S(2)}) copy-start(bf16[128,7168]{1,0:T(8,128)(2,1)} %get-tuple-element.15) | copy-start | bytes 5505028
  186.0 1.2 copy-start.3
  186.0 1.8 copy-start.2

commit v6 on v5

--- a/solution.py
+++ b/solution.py
@@ -259,31 +259,27 @@
                 f_copy(r, way).start()
                 c_copy(r, 1 + way).start()
 
+        @pl.when(r == 0)
+        def _():
+            pass_on(2, chunk(0, 2))
+            pass_on(3, chunk(0, 3))
+
+        @pl.when((r >= 1) & (r + 3 < SHARED))
+        def _():
+            pass_on(r + 3, chunk(0, r + 3))
+
         @pl.when(r + 2 < SHARED)
         def _():
-            pass_on(r + 2, chunk(0, r + 2))
-
-        @pl.when((r >= 1) & (r + 3 < SHARED))
-        def _():
-            start_y(r + 3, chunk(0, r + 3))
+            first(r + 2)
+
+        @pl.when(r == 0)
+        def _():
+            start_y(4, chunk(0, 4))
+            start_y(5, chunk(0, 5))
 
         @pl.when(r < 4)
         def _():
             start_y(SHARED + r, common(r))
-
-        @pl.when(r + 2 < SHARED)
-        def _():
-            first(r + 2)
-
-        @pl.when((r >= 1) & (r < 5))
-        def _():
-            pass_on(SHARED + r - 1, common(r - 1))
-
-        @pl.when((r >= 2) & (r < 6))
-        def _():
-            for way in (0, 1):
-                g_copy(SHARED + r - 2, common(r - 2), way).wait_recv()
-            v_copy(r - 2).start()
 
         @pl.when(r == 1)
         def _():
@@ -302,16 +298,29 @@
         def _():
             multiply_near(r)
 
-        @pl.when((r >= 3) & (r < 7))
-        def _():
-            v_land(r - 3).wait_recv()
-            multiply(common(r - 3), lax.rem(r - 3, 2))
-
         @pl.when((r >= 1) & (r <= SHARED))
         def _():
             for way in (0, 1):
                 f_land(r - 1, way).wait_recv()
             c_copy(r - 1, 3).start()
+
+        @pl.when((r >= 1) & (r < 5))
+        def _():
+            pass_on(SHARED + r - 1, common(r - 1))
+
+        @pl.when((r >= 2) & (r < 6))
+        def _():
+            for way in (0, 1):
+                g_copy(SHARED + r - 2, common(r - 2), way).wait_recv()
+            v_copy(r - 2).start()
+
+        @pl.when((r >= 3) & (r < 7))
+        def _():
+            v_land(r - 3).wait_recv()
+            multiply(common(r - 3), lax.rem(r - 3, 2))
+
+        @pl.when((r >= 1) & (r <= SHARED))
+        def _():
             c_land(chunk(2, r - 1), r - 1, 3).wait_recv()
             multiply(chunk(2, r - 1), lax.rem(r - 1, 2))
 
@@ -386,8 +395,8 @@
 
 
 def moe_kernel(
-    hid_ref, gain_ref, rout_ref, bias_ref, cho_ref, wg_ref, wu_ref, wd_ref,
-    moe_ref, load_ref, next_ref,
+    hid_ref, gain_ref, rout_ref, cho_ref, wg_ref, wu_ref, wd_ref,
+    back_ref, coeff_ref, count_ref,
     wg, wu, wd, rt, normed, gain, snd, land, rows, ybuf, r1, sbuf, half_in, full_in, rsend, ret, cnt, cnt_tp, cnt_ep,
     loc, d_s, d_r, ax_s, ax_r, af_s, af_r, ac_s, ac_r, k_s, k_r, l_s, l_r, rt_s, rt_r, rs_s, rs_r,
     p_s, p_r, h_s, h_r, q_s, q_r, b_s, b_r,
@@ -625,12 +634,7 @@
     counts = cnt_ep[0]
     for i in range(1, 8):
         counts += cnt_ep[i]
-    counts = counts[0:1]
-    slots = 128.0 * 128.0 * TOP
-    load_ref[...] = counts * 256.0 / slots
-    gap = slots - counts * 256.0
-    sign = jnp.where(gap > 0.0, 1.0, jnp.where(gap < 0.0, -1.0, 0.0))
-    next_ref[...] = bias_ref[...] + bias_rate * sign
+    count_ref[...] = counts
 
     for p in tp_peers:
         src = tp_at(*p)
@@ -665,8 +669,7 @@
     weight = jnp.zeros((256, 128), jnp.float32)
     for k in range(TOP):
         weight += jnp.where(cho_ref[k : k + 1, :] == expert, route_scale * chosen[k] / norm_by, 0.0)
-    coeff = jnp.where(pick > 0.0, weight, 0.0).T
-    lane_cut = lax.broadcasted_iota(jnp.int32, (128, 256), 1) % 8
+    coeff_ref[...] = jnp.where(pick > 0.0, weight, 0.0).T
 
     back_row = lax.broadcasted_iota(jnp.int32, (256, 32), 0)
     back_col = lax.broadcasted_iota(jnp.int32, (256, 32), 1)
@@ -690,17 +693,11 @@
     own_back.start()
     for p in tp_peers:
         b_copy(p).start()
-    high = coeff.astype(jnp.bfloat16)
-    low = (coeff - high.astype(jnp.float32)).astype(jnp.bfloat16)
     own_back.wait()
     for p in tp_peers:
         src = tp_at(*p)
         remote(rsend.at[src], ret.at[src], b_s.at[src], b_r.at[src], (src, ep)).wait_recv()
-    back = ret[...].reshape(256, LANE)
-    for j in range(8):
-        mixed = jnp.dot(jnp.where(lane_cut == j, high, 0.0).astype(jnp.bfloat16), back, preferred_element_type=jnp.float32)
-        mixed += jnp.dot(jnp.where(lane_cut == j, low, 0.0).astype(jnp.bfloat16), back, preferred_element_type=jnp.float32)
-        moe_ref[:, cut(j)] = mixed.astype(jnp.bfloat16)
+    back_ref[...] = ret[...]
 
     for p in tp_peers:
         d_copy(p).wait_send()
@@ -723,20 +720,46 @@
             q_copy(n, way).wait_send()
 
 
+def mix_kernel(hid_ref, back_ref, coeff_ref, count_ref, bias_ref, kept_ref, moe_ref, load_ref, next_ref):
+    i = pl.program_id(0)
+    kept_ref[...] = hid_ref[...]
+
+    @pl.when(i == 0)
+    def _():
+        slots = 128.0 * 128.0 * TOP
+        for k in range(2):
+            counts = count_ref[0:1, k * 128 : (k + 1) * 128]
+            load_ref[k : k + 1, :] = counts * 256.0 / slots
+            gap = slots - counts * 256.0
+            sign = jnp.where(gap > 0.0, 1.0, jnp.where(gap < 0.0, -1.0, 0.0))
+            next_ref[k : k + 1, :] = bias_ref[k : k + 1, :] + bias_rate * sign
+
+    back = back_ref[...].reshape(256, LANE)
+    coeff = coeff_ref[...]
+    high = coeff.astype(jnp.bfloat16).astype(jnp.float32)
+    low = coeff - high
+    lane_cut = lax.broadcasted_iota(jnp.int32, (128, 256), 1) % 8
+    for k in range(2):
+        here = lane_cut == 2 * i + k
+        mixed = jnp.dot(jnp.where(here, high, 0.0).astype(jnp.bfloat16), back, preferred_element_type=jnp.float32)
+        mixed += jnp.dot(jnp.where(here, low, 0.0).astype(jnp.bfloat16), back, preferred_element_type=jnp.float32)
+        moe_ref[:, k * LANE : (k + 1) * LANE] = mixed.astype(jnp.bfloat16)
+
+
 def experts(hidden_out, norm_gain, router, router_bias, choices, w_gate, w_up, w_down):
     dma = pltpu.SemaphoreType.DMA
     bf16, f32 = jnp.bfloat16, jnp.float32
     vmem = pl.BlockSpec(memory_space=VMEM)
     anywhere = pl.BlockSpec(memory_space=pl.ANY)
-    moe_out, load, bias_next = pl.pallas_call(
+    back, coeff, counts = pl.pallas_call(
         moe_kernel,
         name="experts",
         out_shape=(
-            jax.ShapeDtypeStruct((128, 7168), bf16),
-            jax.ShapeDtypeStruct((1, 256), f32),
-            jax.ShapeDtypeStruct((1, 256), f32),
+            jax.ShapeDtypeStruct((16, 16, LANE), bf16),
+            jax.ShapeDtypeStruct((128, 256), f32),
+            jax.ShapeDtypeStruct((8, 256), f32),
         ),
-        in_specs=[vmem] * 5 + [anywhere] * 3,
+        in_specs=[vmem] * 4 + [anywhere] * 3,
         out_specs=(vmem,) * 3,
         scratch_shapes=[
             VMEM((7168, 256), bf16), VMEM((7168, 256), bf16), VMEM((256, 7168), bf16),
@@ -754,20 +777,31 @@
             collective_id=1, has_side_effects=True, vmem_limit_bytes=56 * 1024 * 1024
         ),
     )(
-        hidden_out, norm_gain.reshape(-1, 128), router.T, router_bias.reshape(1, -1), choices.T,
+        hidden_out, norm_gain.reshape(-1, 128), router.T, choices.T,
         w_gate[0], w_up[0], w_down[0],
     )
-    return moe_out, load.reshape(-1), bias_next.reshape(-1)
+    block = pl.BlockSpec((128, 2 * LANE), lambda i: (0, i))
+    hidden_kept, moe_out, load, bias_next = pl.pallas_call(
+        mix_kernel,
+        name="mix",
+        grid=(4,),
+        out_shape=(
+            jax.ShapeDtypeStruct((128, 7168), bf16),
+            jax.ShapeDtypeStruct((128, 7168), bf16),
+            jax.ShapeDtypeStruct((2, 128), f32),
+            jax.ShapeDtypeStruct((2, 128), f32),
+        ),
+        in_specs=[block] + [vmem] * 4,
+        out_specs=(block, block, vmem, vmem),
+    )(hidden_out, back, coeff, counts, router_bias.reshape(2, 128))
+    return hidden_kept, moe_out, load.reshape(-1), bias_next.reshape(-1)
 
 
 def on_device(
     attn_out, residual, w_out, norm_gain, router, router_bias, choices, w_gate, w_up, w_down
 ):
     hidden_out = project(attn_out, w_out, residual)
-    moe_out, load, bias_next = experts(
-        hidden_out, norm_gain, router, router_bias, choices, w_gate, w_up, w_down
-    )
-    return (hidden_out, moe_out, load, bias_next)
+    return experts(hidden_out, norm_gain, router, router_bias, choices, w_gate, w_up, w_down)
 
 
 def solution(mesh):

time: 189 us -> 186 us (0.984)
  local copies, waits for them, and re-layouts: 4.51 us -> 0 us
  Pallas kernels: 183 us -> 185 us
    pallas_call x0 -> x1, Pallas kernels: none -> 4.93 us  [experts(): pl.pallas_call(mix_kernel, name='mix', grid=(4,), out_shape=(jax.ShapeDty...]
    unnamed x12 -> x0, local copies, waits for them, and re-layouts: 4.51 us -> none
    pallas_call x1, Pallas kernels: 118 us -> 115 us  [project(): pl.pallas_call(project_kernel, name='project', out_shape=jax.ShapeDtypeSt...]
where the time goes in v6:
time: 186 us
  Pallas kernels  185 us (99%)
    pallas_call x1, Pallas kernels, project(): pl.pallas_call(project_kernel, name='project', out_shape=jax.ShapeDtypeSt...  115 us
    pallas_call x1, Pallas kernels, experts(): pl.pallas_call(moe_kernel, name='experts', out_shape=(jax.ShapeDtypeStruc...  64.7 us
    pallas_call x1, Pallas kernels, experts(): pl.pallas_call(mix_kernel, name='mix', grid=(4,), out_shape=(jax.ShapeDty...  4.93 us

profile of v6, /device:TPU:1, one launch (start us, length us, event | category | flops | bytes accessed | tf_op | source)
XLA Modules:
  0.0 185.5 jit_solution(15986297806608137229)
XLA Ops:
  0.6 115.3 %project.1.hid_ref = bf16[128,7168]{1,0:T(8,128)(2,1)} custom-call(bf16[4,4,128,512]{3,2,1,0:T(8,128)(2,1)} %bitcast.13, bf16[512,7168]{1,0:T(8,128)(2,1)} %w_ref.1, bf16[128,7168]{1,0:T(8,128)(2,1)} %res_ref.1), custom_call_target="tpu_custom_call" | custom-call | tf_op jit(solution)/shard_map/project/pallas_call | solution.py:369
  115.9 64.7 %experts.1 = (bf16[16,16,896]{2,1,0:T(8,128)(2,1)}, f32[128,256]{1,0:T(8,128)}, f32[8,256]{1,0:T(8,128)}) custom-call(bf16[128,7168]{1,0:T(8,128)(2,1)} %project.1.hid_ref, bf16[56,128]{1,0:T(8,128)(2,1)} %bitcast.15, bf16[16,7168]{1,0:T(8,128)(2,1)} %bitcast.14, s32[8,128]{1,0:T(8,128)} %bitcast.16, bf16[7168,256]{1,0:T(8,128)(2,1)} %bitcast.10, ...), custom_call_target="tpu_custom_call" | custom-call | tf_op jit(solution)/shard_map/experts/pallas_call | solution.py:754
  180.6 4.9 %mix.1 = (bf16[128,7168]{1,0:T(8,128)(2,1)}, bf16[128,7168]{1,0:T(8,128)(2,1)}, f32[2,128]{1,0:T(2,128)}, f32[2,128]{1,0:T(2,128)}) custom-call(bf16[128,7168]{1,0:T(8,128)(2,1)} %project.1.hid_ref, bf16[16,16,896]{2,1,0:T(8,128)(2,1)} %get-tuple-element.11.back_ref, f32[128,256]{1,0:T(8,128)} %get-tuple-element.12.coeff_ref, ...), custom_call_target="tpu_custom_call" | custom-call | tf_op jit(solution)/shard_map/mix/pallas_call | solution.py:784

commit v7 on v6

--- a/solution.py
+++ b/solution.py
@@ -16,7 +16,7 @@
 MESH = pl.DeviceIdType.MESH
 VMEM = pltpu.VMEM
 ROUNDS = 7
-SHARED = 6
+SHARED = 5
 CH = 256
 
 
@@ -100,7 +100,7 @@
         )
 
     def common(u):
-        return u * ROUNDS + SHARED
+        return lax.div(u, 2) * ROUNDS + SHARED + lax.rem(u, 2)
 
     def v_copy(u):
         part = wbuf.at[common(u), :, pl.ds(half, 256), :]
@@ -218,9 +218,10 @@
             def _(q):
                 work(near(q, r), lax.rem(r, 2))
 
-        @pl.when((r >= 3) & (r < 7))
-        def _():
-            work(common(r - 3), lax.rem(r - 3, 2))
+        @pl.when((r >= 2) & (r < 6))
+        def _():
+            for k in (0, 1):
+                work(common(2 * r - 4 + k), 1 - k)
 
         @pl.when((r >= 1) & (r <= SHARED))
         def _():
@@ -275,11 +276,11 @@
         @pl.when(r == 0)
         def _():
             start_y(4, chunk(0, 4))
-            start_y(5, chunk(0, 5))
 
         @pl.when(r < 4)
         def _():
-            start_y(SHARED + r, common(r))
+            for k in (0, 1):
+                start_y(SHARED + 2 * r + k, common(2 * r + k))
 
         @pl.when(r == 1)
         def _():
@@ -306,18 +307,23 @@
 
         @pl.when((r >= 1) & (r < 5))
         def _():
-            pass_on(SHARED + r - 1, common(r - 1))
+            for k in (0, 1):
+                pass_on(SHARED + 2 * r - 2 + k, common(2 * r - 2 + k))
 
         @pl.when((r >= 2) & (r < 6))
         def _():
-            for way in (0, 1):
-                g_copy(SHARED + r - 2, common(r - 2), way).wait_recv()
-            v_copy(r - 2).start()
-
-        @pl.when((r >= 3) & (r < 7))
-        def _():
-            v_land(r - 3).wait_recv()
-            multiply(common(r - 3), lax.rem(r - 3, 2))
+            for k in (0, 1):
+                u = 2 * r - 4 + k
+                for way in (0, 1):
+                    g_copy(SHARED + u, common(u), way).wait_recv()
+                v_copy(u).start()
+
+        @pl.when((r >= 2) & (r < 6))
+        def _():
+            for k in (0, 1):
+                u = 2 * r - 4 + k
+                v_land(u).wait_recv()
+                multiply(common(u), 1 - k)
 
         @pl.when((r >= 1) & (r <= SHARED))
         def _():
@@ -349,7 +355,7 @@
         for q in range(4):
             c_copy(r, q).wait_send()
 
-    @pl.loop(0, 4)
+    @pl.loop(0, 8)
     def _(u):
         for way in (0, 1):
             y_copy(SHARED + u, common(u), way).wait_send()
@@ -380,8 +386,8 @@
             VMEM((28, 2, 64, CH), jnp.bfloat16),
             VMEM((28, 2, 128, CH), jnp.bfloat16),
             VMEM((128, 7168), jnp.bfloat16),
-            dma((4,)), dma((2, 4, 3)), dma((2, 4, 3)), dma((10, 2)), dma((10, 2)), dma((10, 2)), dma((10, 2)),
-            dma((4,)), dma((4,)), dma((6, 2)), dma((6, 2)), dma((6, 2)), dma((6, 2)), dma((6, 4)), dma((6, 4)),
+            dma((4,)), dma((2, 4, 3)), dma((2, 4, 3)), dma((13, 2)), dma((13, 2)), dma((13, 2)), dma((13, 2)),
+            dma((8,)), dma((8,)), dma((5, 2)), dma((5, 2)), dma((5, 2)), dma((5, 2)), dma((5, 4)), dma((5, 4)),
             dma((28, 2)), dma((28, 2)), dma((28, 2)), dma((28, 2)),
         ],
         compiler_params=pltpu.CompilerParams(
@@ -736,13 +742,10 @@
 
     back = back_ref[...].reshape(256, LANE)
     coeff = coeff_ref[...]
-    high = coeff.astype(jnp.bfloat16).astype(jnp.float32)
-    low = coeff - high
     lane_cut = lax.broadcasted_iota(jnp.int32, (128, 256), 1) % 8
     for k in range(2):
         here = lane_cut == 2 * i + k
-        mixed = jnp.dot(jnp.where(here, high, 0.0).astype(jnp.bfloat16), back, preferred_element_type=jnp.float32)
-        mixed += jnp.dot(jnp.where(here, low, 0.0).astype(jnp.bfloat16), back, preferred_element_type=jnp.float32)
+        mixed = jnp.dot(jnp.where(here, coeff, 0.0).astype(jnp.bfloat16), back, preferred_element_type=jnp.float32)
         moe_ref[:, k * LANE : (k + 1) * LANE] = mixed.astype(jnp.bfloat16)
 
 

time: 186 us -> 181 us (0.973)
  Pallas kernels: 185 us -> 180 us
    pallas_call x1, Pallas kernels: 115 us -> 110 us  [project(): pl.pallas_call(project_kernel, name='project', out_shape=jax.ShapeDtypeSt...]
where the time goes in v7:
time: 181 us
  Pallas kernels  180 us (99%)
    pallas_call x1, Pallas kernels, project(): pl.pallas_call(project_kernel, name='project', out_shape=jax.ShapeDtypeSt...  110 us
    pallas_call x1, Pallas kernels, experts(): pl.pallas_call(moe_kernel, name='experts', out_shape=(jax.ShapeDtypeStruc...  65.2 us
    pallas_call x1, Pallas kernels, experts(): pl.pallas_call(mix_kernel, name='mix', grid=(4,), out_shape=(jax.ShapeDty...  4.55 us

profile of v7, /device:TPU:1, one launch (start us, length us, event | category | flops | bytes accessed | tf_op | source)
XLA Modules:
  0.0 180.6 jit_solution(10808787918853180687)
XLA Ops:
  0.6 110.2 %project.1.hid_ref = bf16[128,7168]{1,0:T(8,128)(2,1)} custom-call(bf16[4,4,128,512]{3,2,1,0:T(8,128)(2,1)} %bitcast.13, bf16[512,7168]{1,0:T(8,128)(2,1)} %w_ref.1, bf16[128,7168]{1,0:T(8,128)(2,1)} %res_ref.1), custom_call_target="tpu_custom_call" | custom-call | tf_op jit(solution)/shard_map/project/pallas_call | solution.py:375
  110.9 65.2 %experts.1 = (bf16[16,16,896]{2,1,0:T(8,128)(2,1)}, f32[128,256]{1,0:T(8,128)}, f32[8,256]{1,0:T(8,128)}) custom-call(bf16[128,7168]{1,0:T(8,128)(2,1)} %project.1.hid_ref, bf16[56,128]{1,0:T(8,128)(2,1)} %bitcast.15, bf16[16,7168]{1,0:T(8,128)(2,1)} %bitcast.14, s32[8,128]{1,0:T(8,128)} %bitcast.16, bf16[7168,256]{1,0:T(8,128)(2,1)} %bitcast.10, ...), custom_call_target="tpu_custom_call" | custom-call | tf_op jit(solution)/shard_map/experts/pallas_call | solution.py:757
  176.1 4.6 %mix.1 = (bf16[128,7168]{1,0:T(8,128)(2,1)}, bf16[128,7168]{1,0:T(8,128)(2,1)}, f32[2,128]{1,0:T(2,128)}, f32[2,128]{1,0:T(2,128)}) custom-call(bf16[128,7168]{1,0:T(8,128)(2,1)} %project.1.hid_ref, bf16[16,16,896]{2,1,0:T(8,128)(2,1)} %get-tuple-element.11.back_ref, f32[128,256]{1,0:T(8,128)} %get-tuple-element.12.coeff_ref, ...), custom_call_target="tpu_custom_call" | custom-call | tf_op jit(solution)/shard_map/mix/pallas_call | solution.py:787

commit v8 on v7

--- a/solution.py
+++ b/solution.py
@@ -282,6 +282,19 @@
             for k in (0, 1):
                 start_y(SHARED + 2 * r + k, common(2 * r + k))
 
+        @pl.when((r >= 1) & (r < 5))
+        def _():
+            for k in (0, 1):
+                pass_on(SHARED + 2 * r - 2 + k, common(2 * r - 2 + k))
+
+        @pl.when((r >= 2) & (r < 6))
+        def _():
+            for k in (0, 1):
+                u = 2 * r - 4 + k
+                for way in (0, 1):
+                    g_copy(SHARED + u, common(u), way).wait_recv()
+                v_copy(u).start()
+
         @pl.when(r == 1)
         def _():
             for g in range(4):
@@ -291,10 +304,6 @@
                         remote(part, part, a_s.at[kind, g, k], a_r.at[kind, g, k], at(z, y + 1, x, c)).wait_recv()
             multiply_near(0)
 
-        @pl.when(r >= 2)
-        def _():
-            step(combine, r - 1)
-
         @pl.when((r >= 1) & (r < SHARED))
         def _():
             multiply_near(r)
@@ -305,18 +314,9 @@
                 f_land(r - 1, way).wait_recv()
             c_copy(r - 1, 3).start()
 
-        @pl.when((r >= 1) & (r < 5))
-        def _():
-            for k in (0, 1):
-                pass_on(SHARED + 2 * r - 2 + k, common(2 * r - 2 + k))
-
-        @pl.when((r >= 2) & (r < 6))
-        def _():
-            for k in (0, 1):
-                u = 2 * r - 4 + k
-                for way in (0, 1):
-                    g_copy(SHARED + u, common(u), way).wait_recv()
-                v_copy(u).start()
+        @pl.when(r >= 2)
+        def _():
+            step(combine, r - 1)
 
         @pl.when((r >= 2) & (r < 6))
         def _():

time: 181 us -> 178 us (0.983)
  Pallas kernels: 180 us -> 177 us
    pallas_call x1, Pallas kernels: 110 us -> 106 us  [project(): pl.pallas_call(project_kernel, name='project', out_shape=jax.ShapeDtypeSt...]
where the time goes in v8:
time: 178 us; the launch traced here: 177 us
  Pallas kernels  177 us (99%)
    pallas_call x1, Pallas kernels, project(): pl.pallas_call(project_kernel, name='project', out_shape=jax.ShapeDtypeSt...  106 us
    pallas_call x1, Pallas kernels, experts(): pl.pallas_call(moe_kernel, name='experts', out_shape=(jax.ShapeDtypeStruc...  65.9 us
    pallas_call x1, Pallas kernels, experts(): pl.pallas_call(mix_kernel, name='mix', grid=(4,), out_shape=(jax.ShapeDty...  4.57 us

profile of v8, /device:TPU:1, one launch (start us, length us, event | category | flops | bytes accessed | tf_op | source)
XLA Modules:
  0.0 177.3 jit_solution(6126714877255185477)
XLA Ops:
  0.6 106.2 %project.1.hid_ref = bf16[128,7168]{1,0:T(8,128)(2,1)} custom-call(bf16[4,4,128,512]{3,2,1,0:T(8,128)(2,1)} %bitcast.13, bf16[512,7168]{1,0:T(8,128)(2,1)} %w_ref.1, bf16[128,7168]{1,0:T(8,128)(2,1)} %res_ref.1), custom_call_target="tpu_custom_call" | custom-call | tf_op jit(solution)/shard_map/project/pallas_call | solution.py:375
  106.8 65.9 %experts.1 = (bf16[16,16,896]{2,1,0:T(8,128)(2,1)}, f32[128,256]{1,0:T(8,128)}, f32[8,256]{1,0:T(8,128)}) custom-call(bf16[128,7168]{1,0:T(8,128)(2,1)} %project.1.hid_ref, bf16[56,128]{1,0:T(8,128)(2,1)} %bitcast.15, bf16[16,7168]{1,0:T(8,128)(2,1)} %bitcast.14, s32[8,128]{1,0:T(8,128)} %bitcast.16, bf16[7168,256]{1,0:T(8,128)(2,1)} %bitcast.10, ...), custom_call_target="tpu_custom_call" | custom-call | tf_op jit(solution)/shard_map/experts/pallas_call | solution.py:757
  172.8 4.6 %mix.1 = (bf16[128,7168]{1,0:T(8,128)(2,1)}, bf16[128,7168]{1,0:T(8,128)(2,1)}, f32[2,128]{1,0:T(2,128)}, f32[2,128]{1,0:T(2,128)}) custom-call(bf16[128,7168]{1,0:T(8,128)(2,1)} %project.1.hid_ref, bf16[16,16,896]{2,1,0:T(8,128)(2,1)} %get-tuple-element.11.back_ref, f32[128,256]{1,0:T(8,128)} %get-tuple-element.12.coeff_ref, ...), custom_call_target="tpu_custom_call" | custom-call | tf_op jit(solution)/shard_map/mix/pallas_call | solution.py:787

commit v9 on v8

--- a/solution.py
+++ b/solution.py
@@ -233,9 +233,9 @@
     pass_on(1, chunk(0, 1))
     start_a(0)
     start_a(1)
+    start_a(2)
     first(0)
     first(1)
-    start_a(2)
     start_y(2, chunk(0, 2))
     start_y(3, chunk(0, 3))
     start_a(3)
@@ -318,6 +318,16 @@
         def _():
             step(combine, r - 1)
 
+        @pl.when(r == 2)
+        def _():
+            @pl.loop(0, 3)
+            def _(q):
+                combine(near(q, 0), 0)
+
+        @pl.when(r >= 3)
+        def _():
+            step(finish, r - 3)
+
         @pl.when((r >= 2) & (r < 6))
         def _():
             for k in (0, 1):
@@ -329,16 +339,6 @@
         def _():
             c_land(chunk(2, r - 1), r - 1, 3).wait_recv()
             multiply(chunk(2, r - 1), lax.rem(r - 1, 2))
-
-        @pl.when(r == 2)
-        def _():
-            @pl.loop(0, 3)
-            def _(q):
-                combine(near(q, 0), 0)
-
-        @pl.when(r >= 3)
-        def _():
-            step(finish, r - 3)
 
     for g in range(4):
         for e in (1, 2, 3):
@@ -438,11 +438,9 @@
     lane = lax.broadcasted_iota(jnp.int32, (256, 128), 1)
     expert = row // 16
     member = jnp.zeros((256, 128), jnp.float32)
-    named = jnp.zeros((256, 128), jnp.float32)
     for k in range(TOP):
         ck = cho_ref[k : k + 1, :]
         member += jnp.where(ck == expert, 1.0, 0.0)
-        named += jnp.where(ck == row, 1.0, 0.0)
     before = jnp.where(row[:128] < lane[:128], 1.0, 0.0).astype(jnp.bfloat16)
     rank = jnp.dot(member.astype(jnp.bfloat16), before, preferred_element_type=jnp.float32)
     slot = ((row // 8) % 2).astype(jnp.float32)
@@ -461,9 +459,6 @@
     outgoing = picked * lax.rsqrt(ssq / width + norm_eps) * gain[...][None]
     snd[...] = outgoing.astype(jnp.bfloat16).reshape(16, 16, LANE)
     contract_last = (((1,), (1,)), ((), ()))
-    cnt[...] = lax.dot_general(
-        jnp.ones((8, 128), jnp.bfloat16), named.astype(jnp.bfloat16), contract_last, preferred_element_type=jnp.float32
-    )
     pl.semaphore_wait(barrier, len(tp_peers) + len(ep_peers))
 
     def d_copy(p):
@@ -474,6 +469,13 @@
     own_rows.start()
     for p in tp_peers:
         d_copy(p).start()
+
+    named = jnp.zeros((256, 128), jnp.float32)
+    for k in range(TOP):
+        named += jnp.where(cho_ref[k : k + 1, :] == row, 1.0, 0.0)
+    cnt[...] = lax.dot_general(
+        jnp.ones((8, 128), jnp.bfloat16), named.astype(jnp.bfloat16), contract_last, preferred_element_type=jnp.float32
+    )
 
     def k_copy(p):
         peer = tp_at(*p)

time: 178 us -> 178 us (level)
  no operation moved by 1% of the time
where the time goes in v9:
time: 178 us; the launch traced here: 177 us
  Pallas kernels  177 us (99%)
    pallas_call x1, Pallas kernels, project(): pl.pallas_call(project_kernel, name='project', out_shape=jax.ShapeDtypeSt...  107 us
    pallas_call x1, Pallas kernels, experts(): pl.pallas_call(moe_kernel, name='experts', out_shape=(jax.ShapeDtypeStruc...  65 us
    pallas_call x1, Pallas kernels, experts(): pl.pallas_call(mix_kernel, name='mix', grid=(4,), out_shape=(jax.ShapeDty...  4.55 us

profile of v9, /device:TPU:1, one launch (start us, length us, event | category | flops | bytes accessed | tf_op | source)
XLA Modules:
  0.0 177.4 jit_solution(5049269741380141283)
XLA Ops:
  0.6 107.2 %project.1.hid_ref = bf16[128,7168]{1,0:T(8,128)(2,1)} custom-call(bf16[4,4,128,512]{3,2,1,0:T(8,128)(2,1)} %bitcast.13, bf16[512,7168]{1,0:T(8,128)(2,1)} %w_ref.1, bf16[128,7168]{1,0:T(8,128)(2,1)} %res_ref.1), custom_call_target="tpu_custom_call" | custom-call | tf_op jit(solution)/shard_map/project/pallas_call | solution.py:375
  107.9 65.0 %experts.1 = (bf16[16,16,896]{2,1,0:T(8,128)(2,1)}, f32[128,256]{1,0:T(8,128)}, f32[8,256]{1,0:T(8,128)}) custom-call(bf16[128,7168]{1,0:T(8,128)(2,1)} %project.1.hid_ref, bf16[56,128]{1,0:T(8,128)(2,1)} %bitcast.15, bf16[16,7168]{1,0:T(8,128)(2,1)} %bitcast.14, s32[8,128]{1,0:T(8,128)} %bitcast.16, bf16[7168,256]{1,0:T(8,128)(2,1)} %bitcast.10, ...), custom_call_target="tpu_custom_call" | custom-call | tf_op jit(solution)/shard_map/experts/pallas_call | solution.py:759
  172.9 4.5 %mix.1 = (bf16[128,7168]{1,0:T(8,128)(2,1)}, bf16[128,7168]{1,0:T(8,128)(2,1)}, f32[2,128]{1,0:T(2,128)}, f32[2,128]{1,0:T(2,128)}) custom-call(bf16[128,7168]{1,0:T(8,128)(2,1)} %project.1.hid_ref, bf16[16,16,896]{2,1,0:T(8,128)(2,1)} %get-tuple-element.11.back_ref, f32[128,256]{1,0:T(8,128)} %get-tuple-element.12.coeff_ref, ...), custom_call_target="tpu_custom_call" | custom-call | tf_op jit(solution)/shard_map/mix/pallas_call | solution.py:789

commit v10 on v9

--- a/solution.py
+++ b/solution.py
@@ -745,8 +745,8 @@
     back = back_ref[...].reshape(256, LANE)
     coeff = coeff_ref[...]
     lane_cut = lax.broadcasted_iota(jnp.int32, (128, 256), 1) % 8
-    for k in range(2):
-        here = lane_cut == 2 * i + k
+    for k in range(4):
+        here = lane_cut == 4 * i + k
         mixed = jnp.dot(jnp.where(here, coeff, 0.0).astype(jnp.bfloat16), back, preferred_element_type=jnp.float32)
         moe_ref[:, k * LANE : (k + 1) * LANE] = mixed.astype(jnp.bfloat16)
 
@@ -785,11 +785,11 @@
         hidden_out, norm_gain.reshape(-1, 128), router.T, choices.T,
         w_gate[0], w_up[0], w_down[0],
     )
-    block = pl.BlockSpec((128, 2 * LANE), lambda i: (0, i))
+    block = pl.BlockSpec((128, 4 * LANE), lambda i: (0, i))
     hidden_kept, moe_out, load, bias_next = pl.pallas_call(
         mix_kernel,
         name="mix",
-        grid=(4,),
+        grid=(2,),
         out_shape=(
             jax.ShapeDtypeStruct((128, 7168), bf16),
             jax.ShapeDtypeStruct((128, 7168), bf16),

time: 178 us -> 176 us (0.989)
  no operation moved by 1% of the time
where the time goes in v10:
time: 176 us
  Pallas kernels  176 us (100%)
    pallas_call x1, Pallas kernels, project(): pl.pallas_call(project_kernel, name='project', out_shape=jax.ShapeDtypeSt...  107 us
    pallas_call x1, Pallas kernels, experts(): pl.pallas_call(moe_kernel, name='experts', out_shape=(jax.ShapeDtypeStruc...  65 us

profile of v10, /device:TPU:1, one launch (start us, length us, event | category | flops | bytes accessed | tf_op | source)
XLA Modules:
  0.0 176.3 jit_solution(13846614095307324600)
XLA Ops:
  0.6 107.2 %project.1.hid_ref = bf16[128,7168]{1,0:T(8,128)(2,1)} custom-call(bf16[4,4,128,512]{3,2,1,0:T(8,128)(2,1)} %bitcast.13, bf16[512,7168]{1,0:T(8,128)(2,1)} %w_ref.1, bf16[128,7168]{1,0:T(8,128)(2,1)} %res_ref.1), custom_call_target="tpu_custom_call" | custom-call | tf_op jit(solution)/shard_map/project/pallas_call | solution.py:375
  107.9 65.0 %experts.1 = (bf16[16,16,896]{2,1,0:T(8,128)(2,1)}, f32[128,256]{1,0:T(8,128)}, f32[8,256]{1,0:T(8,128)}) custom-call(bf16[128,7168]{1,0:T(8,128)(2,1)} %project.1.hid_ref, bf16[56,128]{1,0:T(8,128)(2,1)} %bitcast.15, bf16[16,7168]{1,0:T(8,128)(2,1)} %bitcast.14, s32[8,128]{1,0:T(8,128)} %bitcast.16, bf16[7168,256]{1,0:T(8,128)(2,1)} %bitcast.10, ...), custom_call_target="tpu_custom_call" | custom-call | tf_op jit(solution)/shard_map/experts/pallas_call | solution.py:759
  172.9 3.4 %mix.1 = (bf16[128,7168]{1,0:T(8,128)(2,1)}, bf16[128,7168]{1,0:T(8,128)(2,1)}, f32[2,128]{1,0:T(2,128)}, f32[2,128]{1,0:T(2,128)}) custom-call(bf16[128,7168]{1,0:T(8,128)(2,1)} %project.1.hid_ref, bf16[16,16,896]{2,1,0:T(8,128)(2,1)} %get-tuple-element.11.back_ref, f32[128,256]{1,0:T(8,128)} %get-tuple-element.12.coeff_ref, ...), custom_call_target="tpu_custom_call" | custom-call | tf_op jit(solution)/shard_map/mix/pallas_call | solution.py:789
